TPU v7x, 256 devices: a whole 4x4x8 slice. The times are simulated.
256 devices in a mesh: row: 8 (over y_hi, x), col: 32 (over z, y_lo, core).
Axes of the slice: x: 4, y: 4 (y_hi: 2, y_lo: 2; y = y_hi * 2 + y_lo), z: 8, core: 2. Of those that a mesh axis runs over, the one named last changes fastest.
Arguments:
- samples: float32 [384, 16384], P(None, ('row', 'col')), may hold values from -6 to 6
- omega: float32 [16384, 16384], P('row', 'col'), may hold values from -0.5 to 3, as said below
Outputs:
- precision: float32 [16384, 16384], P('row', 'col')
Inputs may be any that keep to these rules, and one draw needn't show every extreme that they name: omega is symmetric; its diagonal entries lie between 1 and 3, its other entries are much smaller.
All inputs are finite; a program needn't handle non-finite values.
Results may differ from a plain program's by a relative error of at most 0.0003.
Values sent between devices are 32-bit elements; how exact they have to be, the bound alone decides.
A program may use at most 128 MiB of HBM per device.

v0:
```python
import jax
import jax.numpy as jnp
from jax import lax
from jax.sharding import PartitionSpec as P

ITERS = 2


step_size = 0.01
penalty = 0.25


def from_root(array, axis, root):
    return lax.dynamic_index_in_dim(lax.all_gather(array, axis), root, 0, keepdims=False)


def copy_for_each(array, axis):
    size = lax.axis_size(axis)
    return lax.all_to_all(
        jnp.broadcast_to(array[None], (size, *array.shape)), axis, 0, 0, tiled=True
    )


def over_copies(array, axis):
    everything = copy_for_each(array, axis)
    return jnp.sum(everything, axis=0)


def filled_up(lines, size):
    spare = -lines.shape[0] % size
    if not spare:
        return lines
    return jnp.concatenate([lines, jnp.zeros((spare, *lines.shape[1:]), lines.dtype)])


def total_of(array, axis):
    lines = array.reshape(-1, *array.shape[1:][-1:])
    own = lax.psum_scatter(
        filled_up(lines, lax.axis_size(axis)), axis, scatter_dimension=0, tiled=True
    )
    whole = lax.all_gather(own, axis).reshape(-1, *lines.shape[1:])
    return lax.slice_in_dim(whole, 0, len(lines)).reshape(array.shape)


def contract_rows(left, right):
    return lax.dot_general(left, right, (((0,), (0,)), ((), ())), precision=lax.Precision.HIGHEST)


def body(samples, omega):
    row_width = omega.shape[0]
    col_width = omega.shape[1]
    count = samples.shape[0]
    ratio = lax.axis_size("col") // lax.axis_size("row")
    col_index = lax.axis_index("col")
    row_index = lax.axis_index("row")
    x_panel = lax.all_gather(samples, "col", axis=1, tiled=True)
    offset = col_index % ratio * col_width
    piece = lax.dynamic_slice_in_dim(x_panel, offset, col_width, 1)
    x_block = from_root(piece, "row", col_index // ratio)
    global_rows = row_index * row_width + lax.broadcasted_iota(jnp.int32, (row_width, col_width), 0)
    global_cols = col_index * col_width + lax.broadcasted_iota(jnp.int32, (row_width, col_width), 1)
    on_diag = global_rows == global_cols
    precision = omega
    for turn in range(ITERS):
        partial_cols = jnp.dot(x_panel, precision, precision=lax.Precision.HIGHEST)
        y_cols = over_copies(partial_cols, "row")
        partial_rows = lax.dot_general(
            x_block, precision, (((1,), (1,)), ((), ())), precision=lax.Precision.HIGHEST
        )
        y_rows = total_of(partial_rows, "col")
        cross = contract_rows(x_panel, y_cols) + contract_rows(y_rows, x_block)
        gradient = cross * (0.5 / count)
        safe = jnp.where(on_diag, precision, 1.0)
        gradient = gradient - jnp.where(on_diag, 1.0 / safe, 0.0)
        moved = precision - step_size * gradient
        shrunk = jnp.sign(moved) * jnp.maximum(jnp.abs(moved) - step_size * penalty, 0.0)
        precision = jnp.where(on_diag, moved, shrunk)
    return precision


def solution(mesh):
    in_specs = (P(None, ("row", "col")), P("row", "col"))
    out_specs = P("row", "col")
    return jax.shard_map(body, mesh=mesh, in_specs=in_specs, out_specs=out_specs, check_vma=False)
```

profile of v0, /device:TPU:25, one launch (start us, length us, event | category | flops | bytes accessed | tf_op | source)
XLA Modules:
  0.0 742.6 jit_solution(1701434583506534846)
XLA Ops:
  7.3 70.8 %all-gather.10.cloned.1.call-done = f32[384,2048]{0,1:T(8,128)} async-done(((f32[384,64]{0,1:T(8,128)}), f32[384,2048]{0,1:T(8,128)}) %all-gather.10.cloned.1.call-update) | async-done | bytes 3145744 | tf_op jit(solution)/shard_map/all_gather | solution.py:56
  78.1 2.1 constant_dynamic-slice_fusion.1
  80.2 92.0 %all-gather.12.cloned.1.call-done = f32[3072,512]{0,1:T(8,128)} async-done(((f32[384,512]{0,1:T(8,128)}), f32[3072,512]{0,1:T(8,128)}) %all-gather.12.cloned.1.call-update) | async-done | bytes 6291472 | tf_op jit(solution)/shard_map/all_gather | solution.py:14
  172.3 4.3 copy.30
  178.1 11.7 %fusion.16 = f32[384,2048]{1,0:T(8,128)} fusion(f32[2048,512]{1,0:T(8,128)S(1)} %copy-done.1, f32[1,384,512]{1,0,2:T(1,128)S(1)} %constant_dynamic-slice_fusion), kind=kOutput, calls=%fused_computation.23 | convolution fusion | flops 4831838208 | bytes 8126464 | tf_op jit(solution)/shard_map/dot_general | solution.py:67
  189.8 64.2 %fusion = f32[16,2048]{1,0:T(8,128)S(1)} fusion(f32[384,2048]{1,0:T(8,128)} %fusion.16), kind=kCustom, calls=%all-reduce-scatter | all-reduce-scatter fusion | flops 1048577 | bytes 3277824
  253.9 4.0 collective-permute-start
  258.0 1.9 collective-permute-start.1
  259.9 8.1 %collective-permute-start.7 = (f32[12,2048]{1,0:T(8,128)S(1)}, f32[12,2048]{1,0:T(8,128)S(1)}, u32[]{:S(2)}, u32[]{:S(2)}) collective-permute-start(f32[12,2048]{1,0:T(8,128)S(1)} %slice), channel_id=1, source_target_pairs={{0,8},{1,9},{2,10},{3,11},{4,12},{5,13},{6,14},{7,15},{8,16},{9,17... | collective-permute-start | bytes 294920
  268.0 5.2 collective-permute-start.2
  273.2 2.0 collective-permute-start.3
  275.2 3.7 collective-permute-start.4
  278.9 4.7 collective-permute-start.5
  283.6 3.7 collective-permute-start.6
  288.8 14.7 %concatenate = f32[140,2048]{1,0:T(8,128)} concatenate(f32[12,2048]{1,0:T(8,128)} %copy-done.6, f32[16,2048]{1,0:T(8,128)} %collective-permute-done.6, f32[16,2048]{1,0:T(8,128)} %collective-permute-done.5, f32[16,2048]{1,0:T(8,128)} %collective-permute-done.4, f32[16,2048]{1,0:T(8,128)} %collective-permute-done.3, f32[16,2048]{1,0:T(8,128)} %collective-permute-done.2, ...), dimensions={0} | concatenate | bytes 2293760
  303.5 1.6 dynamic-slice_bitcast_fusion.1
  305.2 12.0 %fusion.22 = f32[384,512]{1,0:T(8,128)S(1)} fusion(f32[384,2048]{0,1:T(8,128)S(1)} %copy-done, f32[2048,512]{1,0:T(8,128)} %param.3), kind=kOutput, calls=%fused_computation.35 | convolution fusion | flops 4831838208 | bytes 8126464 | tf_op jit(solution)/shard_map/dot_general | solution.py:65
  317.1 3.4 broadcast_in_dim.19
  320.6 7.0 all-to-all-start
  327.8 5.4 copy.23
  333.1 76.1 %all-to-all-done = f32[8,384,512]{2,1,0:T(8,128)} async-done(((f32[8,384,512]{2,1,0:T(8,128)}), f32[8,384,512]{2,1,0:T(8,128)}, u32[]{:S(2)}, u32[]{:S(2)}) %all-to-all-start) | async-done | bytes 6291488 | tf_op jit(solution)/shard_map/all_to_all | solution.py:19
  409.2 4.5 reduce_sum.18
  413.8 12.8 %fusion.23 = f32[512,2048]{1,0:T(8,128)} fusion(f32[384,512]{1,0:T(8,128)} %reduce_sum.18, f32[384,2048]{0,1:T(8,128)S(1)} %copy-done), kind=kOutput, calls=%fused_computation.36 | convolution fusion | flops 4831838208 | bytes 8126464 | tf_op jit(solution)/shard_map/dot_general | solution.py:46
  426.6 12.2 %all-gather.14.cloned.1.call-done = f32[32,12,2048]{2,1,0:T(8,128)} async-done(((f32[1,12,2048]{2,1,0:T(8,128)}), f32[32,12,2048]{2,1,0:T(8,128)}) %all-gather.14.cloned.1.call-update) | async-done | bytes 3145744 | tf_op jit(solution)/shard_map/all_gather | solution.py:41
  438.8 4.7 reshape.16
  443.5 13.5 %compare_select_fusion.3 = f32[2048,512]{0,1:T(8,128)S(1)} fusion(f32[2048,512]{0,1:T(8,128)} %copy.23, f32[512,2048]{1,0:T(8,128)} %fusion.23, f32[384,2048]{1,0:T(8,128)} %reshape.16, s32[2048]{0:T(1024)S(1)} %iota_add_fusion, s32[512]{0:T(512)S(1)} %iota_add_fusion.1, f32[1,384,512]{1,0,2:T(1,128)} %copy-done.3), kind=kOutput, calls=%fused_computation.3 | convolution fusion | flops 4847566848 | bytes 16525312 | tf_op jit(solution)/shard_map/dot_general | solution.py:46
  457.0 2.0 copy-done.2
  459.0 7.0 fusion.13
  466.0 63.3 %fusion.1 = f32[16,2048]{1,0:T(8,128)S(1)} fusion(f32[384,2048]{1,0:T(8,128)} %fusion.13), kind=kCustom, calls=%all-reduce-scatter.1 | all-reduce-scatter fusion | flops 1048577 | bytes 3277824
  529.4 1.9 collective-permute-start.10
  532.6 9.4 %collective-permute-start.15 = (f32[12,2048]{1,0:T(8,128)S(1)}, f32[12,2048]{1,0:T(8,128)S(1)}, u32[]{:S(2)}, u32[]{:S(2)}) collective-permute-start(f32[12,2048]{1,0:T(8,128)S(1)} %slice.1), channel_id=1, source_target_pairs={{0,8},{1,9},{2,10},{3,11},{4,12},{5,13},{6,14},{7,15},{8,16},{9,17... | collective-permute-start | bytes 294920
  542.1 5.9 collective-permute-start.12
  548.0 1.9 collective-permute-start.13
  549.9 2.0 collective-permute-start.14
  552.0 3.2 collective-permute-start.8
  555.2 6.0 collective-permute-start.9
  562.6 1.3 collective-permute-done.9
  563.9 14.7 %concatenate.1 = f32[140,2048]{1,0:T(8,128)} concatenate(f32[12,2048]{1,0:T(8,128)} %copy-done.7, f32[16,2048]{1,0:T(8,128)} %copy-done.10, f32[16,2048]{1,0:T(8,128)} %copy-done.9, f32[16,2048]{1,0:T(8,128)} %copy-done.8, f32[16,2048]{1,0:T(8,128)S(1)} %collective-permute-done.11, f32[16,2048]{1,0:T(8,128)S(1)} %collective-permute-done.10, f32[16,2048]{1,0:T(8,128)} %collective-permute-done.9, ...), dimensions={0} | concatenate | bytes 2293760
  578.6 1.6 dynamic-slice_bitcast_fusion
  580.2 9.5 %convolution_bitcast_fusion = f32[384,512]{0,1:T(8,128)} fusion(f32[2048,512]{0,1:T(8,128)} %copy-done.2, f32[384,2048]{0,1:T(8,128)S(1)} %copy-done), kind=kOutput, calls=%fused_computation.18 | convolution fusion | flops 4831838208 | bytes 8126464 | tf_op jit(solution)/shard_map/dot_general | solution.py:65
  589.7 2.3 copy.24
  592.1 1.9 broadcast_in_dim.21
  594.0 100.2 %all_to_all.10 = f32[8,384,512]{2,1,0:T(8,128)} all-to-all(f32[8,384,512]{2,1,0:T(8,128)S(1)} %broadcast_in_dim.21), channel_id=1, replica_groups=mesh['row'=8,'col'=32] {'row'}, dimensions={0} | all-to-all | bytes 12582912 | tf_op jit(solution)/shard_map/all_to_all | solution.py:19
  694.2 4.5 reduce_sum.19
  698.7 12.8 %fusion.24 = f32[512,2048]{1,0:T(8,128)} fusion(f32[384,512]{1,0:T(8,128)} %reduce_sum.19, f32[384,2048]{0,1:T(8,128)S(1)} %copy-done), kind=kOutput, calls=%fused_computation.37 | convolution fusion | flops 4831838208 | bytes 8126464 | tf_op jit(solution)/shard_map/dot_general | solution.py:46
  711.6 4.8 reshape.18
  716.4 14.2 %compare_select_fusion = f32[2048,512]{0,1:T(8,128)} fusion(f32[2048,512]{0,1:T(8,128)} %copy-done.2, f32[512,2048]{1,0:T(8,128)} %fusion.24, f32[384,2048]{1,0:T(8,128)} %reshape.18, s32[2048]{0:T(1024)S(1)} %iota_add_fusion, s32[512]{0:T(512)S(1)} %iota_add_fusion.1, f32[1,384,512]{1,0,2:T(1,128)S(1)} %copy-done.5), kind=kOutput, calls=%fused_computation | convolution fusion | flops 4847566848 | bytes 16525312 | tf_op jit(solution)/shard_map/dot_general | solution.py:46
  730.6 5.3 copy.26
  (56 shorter events, 6.1 us)
Async XLA Ops:
  6.5 71.5 %all-gather.10.cloned.1.call-start = ((), (), s32[]{:S(2)}) async-start(), calls=%async_computation.2 | async-start | bytes 3244032 | tf_op jit(solution)/shard_map/all_gather | solution.py:56
  7.3 165.0 %all-gather.12.cloned.1.call-start = ((), (), s32[]{:S(2)}) async-start(), calls=%async_computation.3 | async-start | bytes 7077888 | tf_op jit(solution)/shard_map/all_gather | solution.py:14
  80.2 358.6 %all-gather.14.cloned.1.call-start = ((), (), s32[]{:S(2)}) async-start(), calls=%async_computation.4 | async-start | bytes 4325376 | tf_op jit(solution)/shard_map/all_gather | solution.py:41
  172.3 5.8 copy-start.1
  177.2 0.9 copy-start.3
  178.1 109.2 %copy-start.12 = (u32[256]{0:T(256)S(1)}, u32[256]{0:T(256)}, u32[]{:S(2)}) copy-start(u32[256]{0:T(256)} %constant.62) | copy-start | bytes 3076
  189.8 115.4 %copy-start = (f32[384,2048]{0,1:T(8,128)S(1)}, f32[384,2048]{0,1:T(8,128)}, u32[]{:S(2)}) copy-start(f32[384,2048]{0,1:T(8,128)} %all-gather.10.cloned.1.call-done) | copy-start | bytes 9437188
  253.9 25.0 %collective-permute-start = (f32[16,2048]{1,0:T(8,128)S(1)}, f32[16,2048]{1,0:T(8,128)S(1)}, u32[]{:S(2)}, u32[]{:S(2)}) collective-permute-start(f32[16,2048]{1,0:T(8,128)S(1)} %fusion), channel_id=1, source_target_pairs={{0,1},{1,2},{2,3},{3,4},{4,5},{5,6},{6,7},{7,8},{8,9},{9,10},{10,1... | collective-permute-start | bytes 393224
  258.0 25.6 %collective-permute-start.1 = (f32[16,2048]{1,0:T(8,128)S(1)}, f32[16,2048]{1,0:T(8,128)S(1)}, u32[]{:S(2)}, u32[]{:S(2)}) collective-permute-start(f32[16,2048]{1,0:T(8,128)S(1)} %fusion), channel_id=1, source_target_pairs={{0,2},{1,3},{2,4},{3,5},{4,6},{5,7},{6,8},{7,9},{8,10},{9,11},{10,... | collective-permute-start | bytes 393224
  259.9 15.3 %collective-permute-start.7 = (f32[12,2048]{1,0:T(8,128)S(1)}, f32[12,2048]{1,0:T(8,128)S(1)}, u32[]{:S(2)}, u32[]{:S(2)}) collective-permute-start(f32[12,2048]{1,0:T(8,128)S(1)} %slice), channel_id=1, source_target_pairs={{0,8},{1,9},{2,10},{3,11},{4,12},{5,13},{6,14},{7,15},{8,16},{9,17... | collective-permute-start | bytes 294920
  268.0 20.5 %collective-permute-start.2 = (f32[16,2048]{1,0:T(8,128)S(1)}, f32[16,2048]{1,0:T(8,128)}, u32[]{:S(2)}, u32[]{:S(2)}) collective-permute-start(f32[16,2048]{1,0:T(8,128)S(1)} %fusion), channel_id=1, source_target_pairs={{0,3},{1,4},{2,5},{3,6},{4,7},{5,8},{6,9},{7,10},{8,11},{9,12},{10... | collective-permute-start | bytes 393224
  273.2 15.3 %collective-permute-start.3 = (f32[16,2048]{1,0:T(8,128)S(1)}, f32[16,2048]{1,0:T(8,128)}, u32[]{:S(2)}, u32[]{:S(2)}) collective-permute-start(f32[16,2048]{1,0:T(8,128)S(1)} %fusion), channel_id=1, source_target_pairs={{0,4},{1,5},{2,6},{3,7},{4,8},{5,9},{6,10},{7,11},{8,12},{9,13},{1... | collective-permute-start | bytes 393224
  275.2 8.4 %copy-start.6 = (f32[12,2048]{1,0:T(8,128)}, f32[12,2048]{1,0:T(8,128)S(1)}, u32[]{:S(2)}) copy-start(f32[12,2048]{1,0:T(8,128)S(1)} %collective-permute-done.7) | copy-start | bytes 294916
  275.2 13.3 %collective-permute-start.4 = (f32[16,2048]{1,0:T(8,128)S(1)}, f32[16,2048]{1,0:T(8,128)}, u32[]{:S(2)}, u32[]{:S(2)}) collective-permute-start(f32[16,2048]{1,0:T(8,128)S(1)} %fusion), channel_id=1, source_target_pairs={{0,5},{1,6},{2,7},{3,8},{4,9},{5,10},{6,11},{7,12},{8,13},{9,14},{... | collective-permute-start | bytes 393224
  278.9 9.6 %collective-permute-start.5 = (f32[16,2048]{1,0:T(8,128)S(1)}, f32[16,2048]{1,0:T(8,128)}, u32[]{:S(2)}, u32[]{:S(2)}) collective-permute-start(f32[16,2048]{1,0:T(8,128)S(1)} %fusion), channel_id=1, source_target_pairs={{0,6},{1,7},{2,8},{3,9},{4,10},{5,11},{6,12},{7,13},{8,14},{9,15},... | collective-permute-start | bytes 393224
  283.6 5.2 collective-permute-start.6
  320.6 88.7 %all-to-all-start = ((f32[8,384,512]{2,1,0:T(8,128)}), f32[8,384,512]{2,1,0:T(8,128)}, u32[]{:S(2)}, u32[]{:S(2)}) async-start(f32[8,384,512]{2,1,0:T(8,128)} %broadcast_in_dim.19), calls=%async_computation | async-start | bytes 12582912 | tf_op jit(solution)/shard_map/all_to_all | solution.py:19
  327.5 384.0 %all-gather.16.cloned.1.call-start = ((), (), s32[]{:S(2)}) async-start(), calls=%async_computation.5 | async-start | bytes 4325376 | tf_op jit(solution)/shard_map/all_gather | solution.py:41
  443.5 15.5 %copy-start.4 = (f32[1,384,512]{1,0,2:T(1,128)S(1)}, f32[1,384,512]{1,0,2:T(1,128)}, u32[]{:S(2)}) copy-start(f32[1,384,512]{1,0,2:T(1,128)} %copy-done.3) | copy-start | bytes 2359300
  457.0 2.0 copy-start.2
  529.4 22.6 %collective-permute-start.10 = (f32[16,2048]{1,0:T(8,128)S(1)}, f32[16,2048]{1,0:T(8,128)S(1)}, u32[]{:S(2)}, u32[]{:S(2)}) collective-permute-start(f32[16,2048]{1,0:T(8,128)S(1)} %fusion.1), channel_id=1, source_target_pairs={{0,3},{1,4},{2,5},{3,6},{4,7},{5,8},{6,9},{7,10},{8,11},{9,12},{10... | collective-permute-start | bytes 393224
  531.3 23.9 %collective-permute-start.11 = (f32[16,2048]{1,0:T(8,128)S(1)}, f32[16,2048]{1,0:T(8,128)S(1)}, u32[]{:S(2)}, u32[]{:S(2)}) collective-permute-start(f32[16,2048]{1,0:T(8,128)S(1)} %fusion.1), channel_id=1, source_target_pairs={{0,4},{1,5},{2,6},{3,7},{4,8},{5,9},{6,10},{7,11},{8,12},{9,13},{1... | collective-permute-start | bytes 393224
  532.6 17.3 %collective-permute-start.15 = (f32[12,2048]{1,0:T(8,128)S(1)}, f32[12,2048]{1,0:T(8,128)S(1)}, u32[]{:S(2)}, u32[]{:S(2)}) collective-permute-start(f32[12,2048]{1,0:T(8,128)S(1)} %slice.1), channel_id=1, source_target_pairs={{0,8},{1,9},{2,10},{3,11},{4,12},{5,13},{6,14},{7,15},{8,16},{9,17... | collective-permute-start | bytes 294920
  542.1 19.1 %collective-permute-start.12 = (f32[16,2048]{1,0:T(8,128)S(1)}, f32[16,2048]{1,0:T(8,128)S(1)}, u32[]{:S(2)}, u32[]{:S(2)}) collective-permute-start(f32[16,2048]{1,0:T(8,128)S(1)} %fusion.1), channel_id=1, source_target_pairs={{0,5},{1,6},{2,7},{3,8},{4,9},{5,10},{6,11},{7,12},{8,13},{9,14},{... | collective-permute-start | bytes 393224
  548.0 13.2 %collective-permute-start.13 = (f32[16,2048]{1,0:T(8,128)S(1)}, f32[16,2048]{1,0:T(8,128)S(1)}, u32[]{:S(2)}, u32[]{:S(2)}) collective-permute-start(f32[16,2048]{1,0:T(8,128)S(1)} %fusion.1), channel_id=1, source_target_pairs={{0,6},{1,7},{2,8},{3,9},{4,10},{5,11},{6,12},{7,13},{8,14},{9,15},... | collective-permute-start | bytes 393224
  549.9 11.3 %copy-start.7 = (f32[12,2048]{1,0:T(8,128)}, f32[12,2048]{1,0:T(8,128)S(1)}, u32[]{:S(2)}) copy-start(f32[12,2048]{1,0:T(8,128)S(1)} %collective-permute-done.15) | copy-start | bytes 294916
  549.9 11.3 %collective-permute-start.14 = (f32[16,2048]{1,0:T(8,128)S(1)}, f32[16,2048]{1,0:T(8,128)S(1)}, u32[]{:S(2)}, u32[]{:S(2)}) collective-permute-start(f32[16,2048]{1,0:T(8,128)S(1)} %fusion.1), channel_id=1, source_target_pairs={{0,7},{1,8},{2,9},{3,10},{4,11},{5,12},{6,13},{7,14},{8,15},{9,16}... | collective-permute-start | bytes 393224
  552.0 9.3 %collective-permute-start.8 = (f32[16,2048]{1,0:T(8,128)S(1)}, f32[16,2048]{1,0:T(8,128)S(1)}, u32[]{:S(2)}, u32[]{:S(2)}) collective-permute-start(f32[16,2048]{1,0:T(8,128)S(1)} %fusion.1), channel_id=1, source_target_pairs={{0,1},{1,2},{2,3},{3,4},{4,5},{5,6},{6,7},{7,8},{8,9},{9,10},{10,1... | collective-permute-start | bytes 393224
  555.2 8.7 %collective-permute-start.9 = (f32[16,2048]{1,0:T(8,128)S(1)}, f32[16,2048]{1,0:T(8,128)}, u32[]{:S(2)}, u32[]{:S(2)}) collective-permute-start(f32[16,2048]{1,0:T(8,128)S(1)} %fusion.1), channel_id=1, source_target_pairs={{0,2},{1,3},{2,4},{3,5},{4,6},{5,7},{6,8},{7,9},{8,10},{9,11},{10,... | collective-permute-start | bytes 393224
  561.2 0.7 copy-start.8
  561.2 0.7 copy-start.9
  561.2 0.7 copy-start.10
  561.9 0.6 copy-start.11
  711.6 4.8 copy-start.5
Sparse Core Ops, SparseCore 0:
  9.2 68.8 all-gather.9
  80.6 91.5 all-gather.11
  305.3 133.4 all-gather.13
  580.3 126.7 all-gather.15
where the time goes:
time: 755 us; the launch traced here: 743 us
  waiting for transfers between devices  254 us (34%)
  blocking collectives  228 us (30%)
  matrix products  93.6 us (12%)
  starting transfers between devices  72.2 us (10%)
  local copies, waits for them, and re-layouts  72.2 us (10%)
  between operations  14.3 us (2%)
  other arithmetic  9.09 us (1%)
    unnamed x2, blocking collectives  128 us
    all_to_all x1, blocking collectives, copy_for_each(): lax.all_to_all(jnp.broadcast_to(array[None], (size, *array.shape)), axis,...  100 us
    all_gather x1, waiting for transfers between devices, from_root(): lax.all_gather(array, axis)  92 us
    all_to_all x1, waiting for transfers between devices, copy_for_each(): lax.all_to_all(jnp.broadcast_to(array[None], (size, *array.shape)), axis,...  76.1 us
    all_gather x1, waiting for transfers between devices, body(): x_panel = lax.all_gather(samples, 'col', axis=1, tiled=True)  70.8 us
    unnamed x16, starting transfers between devices  65 us
    unnamed x37, local copies, waits for them, and re-layouts  56.5 us
    dot_general x4, matrix products, contract_rows(): lax.dot_general(left, right, (((0,), (0,)), ((), ())), precision=lax.Prec...  53.4 us
  transfers between devices with their start and end apart: 21, of which 6 were waited for; matrix products, arithmetic and copies ran while one was open for 9% of the time, Pallas kernels for 0%

commit v1 on v0

v1 whole, which is shorter than its diff:
```python
import functools

import jax
import jax.numpy as jnp
from jax import lax
from jax.experimental import pallas as pl
from jax.experimental.pallas import tpu as pltpu
from jax.sharding import PartitionSpec as P

ITERS = 2
STEP = 0.01
PENALTY = 0.25
S = 384
EARLY = 128
MESH = pl.DeviceIdType.MESH
F32 = jnp.float32
BF16 = jnp.bfloat16
VMEM_LIMIT = 56 * 2**20


def place():
    r = lax.axis_index("row")
    c = lax.axis_index("col")
    return r % 4, (r // 4) * 2 + (c // 2) % 2, c // 4, c % 2


def device(x, y, z, k):
    return (y // 2) * 4 + x, z * 4 + (y % 2) * 2 + k


def rows(start, size):
    return pl.ds(pl.multiple_of(start, 64), size)


class Copies:
    def __init__(self, send, recv):
        self.send, self.recv = send, recv
        self.pending = []

    def make(self, slot, src, dst, to):
        return pltpu.make_async_remote_copy(
            src_ref=src, dst_ref=dst, send_sem=self.send.at[slot], recv_sem=self.recv.at[slot],
            device_id=to, device_id_type=MESH)

    def start(self, slot, src, dst, to):
        copy = self.make(slot, src, dst, to)
        copy.start()
        self.pending.append((copy, None))
        return copy

    def start_if(self, cond, slot, src, dst, to, send=None):
        copy = pltpu.make_async_remote_copy(
            src_ref=src, dst_ref=dst, send_sem=self.send.at[slot if send is None else send],
            recv_sem=self.recv.at[slot], device_id=to, device_id_type=MESH)

        @pl.when(cond)
        def _():
            copy.start()

        self.pending.append((copy, cond))

    def finish(self):
        for copy, cond in self.pending:
            if cond is None:
                copy.wait_send()
            else:
                @pl.when(cond)
                def _():
                    copy.wait_send()


def greet(partners):
    barrier = pltpu.get_barrier_semaphore()
    for partner in partners:
        pl.semaphore_signal(barrier, inc=1, device_id=partner, device_id_type=MESH)
    pl.semaphore_wait(barrier, len(partners))


def column_piece(buf, x, y, d, e=0):
    return buf.at[rows((((y + e) % 4) // 2 * 4 + (x + 4 - d) % 4) * 64, 64)]


AROUND = (1, 3, 2)


def column_start(cp, buf, x, y, z, k, base):
    mine = column_piece(buf, x, y, 0)
    for d in AROUND:
        cp.start(base + d, mine, mine, device((x + d) % 4, y, z, k))
    cp.start(base, mine, mine, device(x, (y + 2) % 4, z, k))


def column_middle(cp, buf, x, y, z, k, base):
    theirs = column_piece(buf, x, y, 0, 2)
    cp.make(base, theirs, theirs, (0, 0)).wait_recv()
    for d in AROUND:
        cp.start(base + 3 + d, theirs, theirs, device((x + d) % 4, y, z, k))


def column_end(cp, buf, x, y, z, k, base):
    mine = column_piece(buf, x, y, 0)
    for d in AROUND:
        cp.make(base + d, mine, mine, (0, 0)).wait_recv()
        cp.make(base + 3 + d, mine, mine, (0, 0)).wait_recv()


def gather_samples_kernel(own_ref, panel, block, send, recv, sem):
    x, y, z, k = place()
    yl, yh = y % 2, y // 2
    r, c = yh * 4 + x, z * 4 + yl * 2 + k
    up = device(x, y, (z + 1) % 8, k)
    down = device(x, y, (z + 7) % 8, k)
    lo = device(x, yh * 2 + 1 - yl, z, k)
    core = device(x, y, z, 1 - k)
    to_r, to_c = c % 8, r * 4 + c // 8
    own_b = c * 8 + r
    from_r, from_c = own_b // 32, own_b % 32
    moves = (to_r * 32 + to_c) != (r * 32 + c)
    group = [device((x + d) % 4, (y + e) % 4, z, k) for d in range(4) for e in (0, 2) if d or e]
    cp = Copies(send, recv)

    barrier = pltpu.get_barrier_semaphore()
    partners = [up, down, lo, core] + group
    for partner in partners:
        pl.semaphore_signal(barrier, inc=1, device_id=partner, device_id_type=MESH)

    @pl.when(moves)
    def _():
        pl.semaphore_signal(barrier, inc=1, device_id=(from_r, from_c), device_id_type=MESH)

    def at(zz, l):
        return panel.at[rows((zz * 4 + l * 2 + k) * 64, 64)]

    def early(ref):
        return ref.at[:, pl.ds(0, EARLY)]

    def late(ref):
        return ref.at[:, pl.ds(EARLY, S - EARLY)]

    panel[rows(c * 64, 64)] = own_ref[...]
    pl.semaphore_wait(barrier, len(partners) + jnp.where(moves, 1, 0))

    own = at(z, yl)
    E_OWN, UP, DOWN, UP_E, DOWN_E, LO, CORE, CORE_LO, COL = 0, 1, 5, 8, 12, 16, 24, 32, 40
    PERM = 47
    cp.start(E_OWN, early(own), early(own), lo)
    cp.start(UP, own, own, up)
    cp.start(DOWN, own, own, down)
    cp.start_if(moves, PERM, own, block.at[rows(to_r * 64, 64)], (to_r, to_c))

    @pl.when(jnp.logical_not(moves))
    def _():
        block[rows(r * 64, 64)] = own_ref[...]

    cp.start(LO, late(own), late(own), lo)
    cp.start(CORE, own, own, core)
    cp.make(E_OWN, early(own), early(own), lo).wait_recv()
    e = early(at(z, 1 - yl))
    cp.start(UP_E, e, e, up)
    cp.start(DOWN_E, e, e, down)

    def lo_arrived(i, zz):
        piece = at(zz, 1 - yl)
        cp.make(LO + i, late(piece), late(piece), lo).wait_recv()
        cp.start(CORE_LO + i, piece, piece, core)

    n = 1
    for t in range(1, 5):
        a = at((z + 8 - t) % 8, yl)
        b = at((z + t) % 8, yl)
        cp.make(UP + t - 1, a, a, up).wait_recv()
        if t < 4:
            cp.start(UP + t, a, a, up)
            cp.make(DOWN + t - 1, b, b, down).wait_recv()
            if t < 3:
                cp.start(DOWN + t, b, b, down)
        ea = early(at((z + 8 - t) % 8, 1 - yl))
        eb = early(at((z + t) % 8, 1 - yl))
        if t < 4:
            cp.make(UP_E + t - 1, ea, ea, up).wait_recv()
            if t < 3:
                cp.start(UP_E + t, ea, ea, up)
        cp.make(DOWN_E + t - 1, eb, eb, down).wait_recv()
        if t < 4:
            cp.start(DOWN_E + t, eb, eb, down)
        cp.start(LO + 2 * t - 1, late(a), late(a), lo)
        cp.start(CORE + 2 * t - 1, a, a, core)
        if t < 4:
            cp.start(LO + 2 * t, late(b), late(b), lo)
            cp.start(CORE + 2 * t, b, b, core)
        if t == 2:
            @pl.when(moves)
            def _():
                cp.make(PERM, own, own, lo).wait_recv()

            column_start(cp, block, x, y, z, k, COL)
        if t == 3:
            column_middle(cp, block, x, y, z, k, COL)
        if t == 1:
            lo_arrived(0, z)
        else:
            lo_arrived(2 * t - 3, (z + 8 - (t - 1)) % 8)
            lo_arrived(2 * t - 2, (z + t - 1) % 8)
    lo_arrived(7, (z + 4) % 8)
    column_end(cp, block, x, y, z, k, COL)
    for i in range(8):
        cp.make(CORE + i, own, own, core).wait_recv()
        cp.make(CORE_LO + i, own, own, core).wait_recv()
    cp.finish()


HALVES = 2
CHUNK = 64 // HALVES
CHUNKS = 4 * HALVES


def gather_projected_kernel(part, panel_out, block, panel, inbox, send, recv, sem):
    x, y, z, k = place()
    yl, yh = y % 2, y // 2
    r = yh * 4 + x
    up = device(x, y, (z + 1) % 8, k)
    down = device(x, y, (z + 7) % 8, k)
    lo = device(x, yh * 2 + 1 - yl, z, k)
    far = device(x, 3 - y, z, k)
    core = device(x, y, z, 1 - k)
    group = [((x + d) % 4, (y + e) % 4) for d in (2, 1, 3, 0) for e in (2, 0) if d or e]
    cp = Copies(send, recv)
    greet([up, down, lo, far, core] + [device(tx, ty, z, k) for tx, ty in group])

    for i, (tx, ty) in enumerate(group):
        tr = (ty // 2) * 4 + tx
        cp.start(i, part.at[rows(tr * 64, 64)], inbox.at[i], device(tx, ty, z, k))
    total = part[rows(r * 64, 64)]
    for i in range(7):
        cp.make(i, inbox.at[i], inbox.at[i], core).wait_recv()
        total = total + inbox[i]
    block[rows(r * 64, 64)] = total
    COL = 7
    column_start(cp, block, x, y, z, k, COL)

    lane = (yl * 2 + k) * 512
    flane = ((1 - yl) * 2 + k) * 512
    fyh = 1 - yh

    def within(h, q):
        d = (0,) + AROUND
        return h * 256 + (x + 4 - d[q // HALVES]) % 4 * 64 + q % HALVES * CHUNK

    def full(base, h, q):
        return panel.at[pl.ds(pl.multiple_of(base + within(h, q), CHUNK), CHUNK)]

    def early(ref):
        return ref.at[:, pl.ds(0, EARLY)]

    def late(ref):
        return ref.at[:, pl.ds(EARLY, S - EARLY)]

    d0 = (z + 8 - x) % 8
    near = jnp.where(jnp.logical_or(d0 <= 2, d0 >= 6), 0, 1)
    other = 1 - near
    Z = 14
    ZD = Z + 4 * CHUNKS
    FAR = ZD + 4 * CHUNKS
    LO = FAR + 2 * CHUNKS
    LOF = LO + CHUNKS
    CORE = LOF + CHUNKS

    def relay(s, q):
        d = (d0 + 4 * s) % 8
        mine = s == yh
        base = jnp.where(mine, lane, 2048)
        a, b = full(base, yh, q), early(full(base, fyh, q))
        slot = Z + (s * CHUNKS + q) * 2

        @pl.when(d == 0)
        def _():
            at = pl.ds(pl.multiple_of(within(yh, q), CHUNK), CHUNK)
            to = pl.ds(pl.multiple_of(base + within(yh, q), CHUNK), CHUNK)
            panel[to] = block[at]

        @pl.when(d != 0)
        def _():
            cp.make(slot, a, a, up).wait_recv()

        cp.start_if(d <= 3, slot, a, a, up)
        cp.start_if(jnp.logical_or(d == 0, d >= 6), slot, a, a, down, slot + ZD - Z)
        la, lb = full(lane, yh, q), early(full(lane, fyh, q))
        theirs = jnp.logical_not(mine)
        cp.start_if(theirs, FAR + 2 * q, a, la, far)
        cp.start_if(mine, LO + q, late(la), late(la), lo)
        cp.start_if(mine, CORE + q, la, la, core)

        @pl.when(d == 0)
        def _():
            at = pl.ds(pl.multiple_of(within(fyh, q), CHUNK), CHUNK)
            to = pl.ds(pl.multiple_of(base + within(fyh, q), CHUNK), CHUNK)
            panel[to, :EARLY] = block[at, :EARLY]

        @pl.when(d != 0)
        def _():
            cp.make(slot + 1, b, b, up).wait_recv()

        cp.start_if(d <= 2, slot + 1, b, b, up)
        cp.start_if(jnp.logical_or(d == 0, d >= 5), slot + 1, b, b, down, slot + 1 + ZD - Z)
        cp.start_if(theirs, FAR + 2 * q + 1, b, lb, far)

    def far_in(q):
        a, b = full(flane, fyh, q), early(full(flane, yh, q))
        cp.make(FAR + 2 * q, a, a, far).wait_recv()
        cp.start(LOF + q, late(a), late(a), lo)
        cp.start(CORE + CHUNKS + q, a, a, core)
        cp.make(FAR + 2 * q + 1, b, b, far).wait_recv()

    def lo_in(q):
        a = full(flane, yh, q)
        cp.make(LO + q, late(a), late(a), lo).wait_recv()
        cp.start(CORE + 2 * CHUNKS + q, a, a, core)

    def lof_in(q):
        a = full(lane, fyh, q)
        cp.make(LOF + q, late(a), late(a), lo).wait_recv()
        cp.start(CORE + 3 * CHUNKS + q, a, a, core)

    piece = column_piece(block, x, y, 0)
    column_middle(cp, block, x, y, z, k, COL)
    for q in range(CHUNKS + 4):
        if q < CHUNKS:
            if q % HALVES == 0 and q:
                d = AROUND[q // HALVES - 1]
                cp.make(COL + d, piece, piece, core).wait_recv()
                cp.make(COL + 3 + d, piece, piece, core).wait_recv()
            relay(near, q)
        if 2 <= q < CHUNKS + 2:
            relay(other, q - 2)
        if 3 <= q < CHUNKS + 3:
            far_in(q - 3)
            lo_in(q - 3)
        if 4 <= q < CHUNKS + 4:
            lof_in(q - 4)
    for g in range(4):
        for q in range(CHUNKS):
            ref = full(lane, yh, q)
            cp.make(CORE + g * CHUNKS + q, ref, ref, core).wait_recv()
    cp.finish()
    out = pltpu.make_async_copy(panel.at[pl.ds(0, 2048)], panel_out, sem)
    out.start()
    out.wait()


def split(a):
    hi = a.astype(BF16)
    return hi, (a - hi.astype(F32)).astype(BF16)


def dot3(ah, al, bh, bl, dims):
    d = lambda p, q: lax.dot_general(p, q, (dims, ((), ())), preferred_element_type=F32)
    return d(ah, bh) + (d(ah, bl) + d(al, bh))


TILE = 256
NN = ((1,), (0,))
NT = ((1,), (1,))


def first_partial_kernel(panel, omega, xh_out, xl_out, part, acc):
    i = pl.program_id(0)
    xh, xl = split(panel[...].T)
    xh_out[...] = xh
    xl_out[...] = xl
    oh, ol = split(omega[...])

    @pl.when(i == 0)
    def _():
        acc[...] = jnp.zeros_like(acc)

    acc[...] += dot3(xh, xl, oh, ol, NN)

    @pl.when(i == pl.num_programs(0) - 1)
    def _():
        part[...] = acc[...].T


def update_kernel(last, count, xr, yr, xc, yc, omega, xh, xl, *rest):
    if last:
        out, rh, rl = rest
    else:
        out, part, rh, rl, acc = rest
    i = pl.program_id(0)
    row0 = lax.axis_index("row") * 2048 + i * TILE
    col0 = lax.axis_index("col") * 512

    @pl.when(i == 0)
    def _():
        h, l = split(yc[...])
        rh[:, :S] = h
        rl[:, :S] = l
        h, l = split(xc[...])
        rh[:, S:] = h
        rl[:, S:] = l
        if not last:
            acc[...] = jnp.zeros_like(acc)

    ah, al = split(jnp.concatenate([xr[...], yr[...]], axis=1))
    cross = dot3(ah, al, rh[...], rl[...], NT)
    old = omega[...]
    moved = old - (STEP * 0.5 / count) * cross
    thr = STEP * PENALTY
    new = moved - jnp.clip(moved, -thr, thr)
    out[...] = new

    @pl.when(jnp.logical_and(row0 < col0 + 512, col0 < row0 + TILE))
    def _():
        gr = row0 + lax.broadcasted_iota(jnp.int32, (TILE, 512), 0)
        gc = col0 + lax.broadcasted_iota(jnp.int32, (TILE, 512), 1)
        on = gr == gc
        safe = jnp.where(on, old, 1.0)
        out[...] = jnp.where(on, moved + STEP / safe, new)

    if not last:
        nh, nl = split(out[...])
        acc[...] += dot3(xh[...], xl[...], nh, nl, NN)

        @pl.when(i == pl.num_programs(0) - 1)
        def _():
            part[...] = acc[...].T


def shape(*dims, dtype=F32):
    return jax.ShapeDtypeStruct(dims, dtype)


def vm():
    return pl.BlockSpec(memory_space=pltpu.VMEM)


def gather_samples(own):
    n = 48
    return pl.pallas_call(
        gather_samples_kernel,
        out_shape=(shape(2048, S), shape(512, S)),
        in_specs=[vm()], out_specs=(vm(), vm()),
        scratch_shapes=[pltpu.SemaphoreType.DMA((n,)), pltpu.SemaphoreType.DMA((n,)), pltpu.SemaphoreType.DMA],
        compiler_params=pltpu.CompilerParams(collective_id=0, has_side_effects=True, vmem_limit_bytes=VMEM_LIMIT),
        name="gather_samples",
    )(own)


def gather_projected(part):
    n = 14 + 16 * CHUNKS
    return pl.pallas_call(
        gather_projected_kernel,
        out_shape=(shape(2048, S), shape(512, S)),
        in_specs=[vm()], out_specs=(vm(), vm()),
        scratch_shapes=[pltpu.VMEM((2560, S), F32), pltpu.VMEM((7, 64, S), F32),
                        pltpu.SemaphoreType.DMA((n,)), pltpu.SemaphoreType.DMA((n,)), pltpu.SemaphoreType.DMA],
        compiler_params=pltpu.CompilerParams(collective_id=1, has_side_effects=True, vmem_limit_bytes=VMEM_LIMIT),
        name="gather_projected",
    )(part)


def first_partial(panel, omega):
    return pl.pallas_call(
        first_partial_kernel,
        grid=(2048 // TILE,),
        out_shape=(shape(S, 2048, dtype=BF16), shape(S, 2048, dtype=BF16), shape(512, S)),
        in_specs=[pl.BlockSpec((TILE, S), lambda i: (i, 0)), pl.BlockSpec((TILE, 512), lambda i: (i, 0))],
        out_specs=(pl.BlockSpec((S, TILE), lambda i: (0, i)), pl.BlockSpec((S, TILE), lambda i: (0, i)),
                   pl.BlockSpec((512, S), lambda i: (0, 0))),
        scratch_shapes=[pltpu.VMEM((S, 512), F32)],
        compiler_params=pltpu.CompilerParams(vmem_limit_bytes=VMEM_LIMIT),
        name="first_partial",
    )(panel, omega)


def update(last, xr, yr, xc, yc, omega, xh, xl):
    tile = pl.BlockSpec((TILE, S), lambda i: (i, 0))
    whole = pl.BlockSpec((512, S), lambda i: (0, 0))
    square = pl.BlockSpec((TILE, 512), lambda i: (i, 0))
    tall = pl.BlockSpec((S, TILE), lambda i: (0, i))
    scratch = [pltpu.VMEM((512, 2 * S), BF16), pltpu.VMEM((512, 2 * S), BF16)]
    if last:
        out_shape, out_specs = shape(2048, 512), square
    else:
        out_shape, out_specs = (shape(2048, 512), shape(512, S)), (square, whole)
        scratch.append(pltpu.VMEM((S, 512), F32))
    return pl.pallas_call(
        functools.partial(update_kernel, last, S),
        grid=(2048 // TILE,),
        out_shape=out_shape,
        in_specs=[tile, tile, whole, whole, square, tall, tall],
        out_specs=out_specs,
        scratch_shapes=scratch,
        compiler_params=pltpu.CompilerParams(vmem_limit_bytes=VMEM_LIMIT),
        name="update_last" if last else "update",
    )(xr, yr, xc, yc, omega, xh, xl)


def body(samples, omega):
    own = samples.T
    xr, xc = gather_samples(own)
    xh, xl, part = first_partial(xr, omega)
    yr, yc = gather_projected(part)
    omega, part = update(False, xr, yr, xc, yc, omega, xh, xl)
    yr, yc = gather_projected(part)
    return update(True, xr, yr, xc, yc, omega, xh, xl)


def solution(mesh):
    in_specs = (P(None, ("row", "col")), P("row", "col"))
    out_specs = P("row", "col")
    return jax.shard_map(body, mesh=mesh, in_specs=in_specs, out_specs=out_specs, check_vma=False)
```

time: 755 us -> 331 us (0.44); the launches traced: 743 us -> 329 us
  Pallas kernels: 0 us -> 329 us
  waiting for transfers between devices: 254 us -> 0 us
  blocking collectives: 228 us -> 0 us
  matrix products: 93.6 us -> 0 us
  local copies, waits for them, and re-layouts: 72.2 us -> 0 us
  starting transfers between devices: 72.2 us -> 0 us
  between operations: 14.3 us -> 0.03 us
  other arithmetic: 9.09 us -> 0 us
    pallas_call x0 -> x6, Pallas kernels: none -> 329 us  [the longest x2 248 us: gather_projected(): pl.pallas_call(gather_projected_kernel, out_shape=(shape(2048, S), shape(...]
    all_gather x4 -> x0, waiting for transfers between devices: 175 us -> none  [the longest x1 92 us: from_root(): lax.all_gather(array, axis)]
    unnamed x2 -> x0, blocking collectives: 128 us -> none
    all_to_all x1 -> x0, blocking collectives: 100 us -> none  [copy_for_each(): lax.all_to_all(jnp.broadcast_to(array[None], (size, *array.shape)), axis,...]
    dot_general x8 -> x0, matrix products: 93.6 us -> none  [the longest x4 53.4 us: contract_rows(): lax.dot_general(left, right, (((0,), (0,)), ((), ())), precision=lax.Prec...]
    all_to_all x1 -> x0, waiting for transfers between devices: 76.1 us -> none  [copy_for_each(): lax.all_to_all(jnp.broadcast_to(array[None], (size, *array.shape)), axis,...]
    unnamed x16 -> x0, starting transfers between devices: 65 us -> none
    unnamed x37 -> x0, local copies, waits for them, and re-layouts: 56.5 us -> none
  transfers between devices with their start and end apart: 21 -> 0, of which waited for: 6 -> 0; matrix products, arithmetic and copies ran while one was open for 9% -> 0% of each run, Pallas kernels for 0% -> 0%
where the time goes in v1:
time: 331 us; the launch traced here: 329 us
  Pallas kernels  329 us (99%)
    pallas_call x2, Pallas kernels, gather_projected(): pl.pallas_call(gather_projected_kernel, out_shape=(shape(2048, S), shape(...  248 us
    pallas_call x1, Pallas kernels, gather_samples(): pl.pallas_call(gather_samples_kernel, out_shape=(shape(2048, S), shape(51...  42.2 us
    pallas_call x2, Pallas kernels, update(): pl.pallas_call(functools.partial(update_kernel, last, S), grid=(2048 // T...  28.5 us
    pallas_call x1, Pallas kernels, first_partial(): pl.pallas_call(first_partial_kernel, grid=(2048 // TILE,), out_shape=(sha...  10.2 us

profile of v1, /device:TPU:25, one launch (start us, length us, event | category | flops | bytes accessed | tf_op | source)
XLA Modules:
  0.0 329.1 jit_solution(15744675460081916896)
XLA Ops:
  0.0 42.2 %gather_samples.1 = (f32[2048,384]{1,0:T(8,128)}, f32[512,384]{1,0:T(8,128)}) custom-call(f32[64,384]{1,0:T(8,128)} %bitcast.1), custom_call_target="tpu_custom_call" | custom-call | tf_op jit(solution)/shard_map/gather_samples/pallas_call | solution.py:438
  42.2 10.2 %first_partial.1 = (bf16[384,2048]{1,0:T(8,128)(2,1)}, bf16[384,2048]{1,0:T(8,128)(2,1)}, f32[512,384]{1,0:T(8,128)}) custom-call(f32[2048,384]{1,0:T(8,128)} %get-tuple-element.16.panel.xr, f32[2048,512]{1,0:T(8,128)} %omega.3), custom_call_target="tpu_custom_call" | custom-call | tf_op jit(solution)/shard_map/first_partial/pallas_call | solution.py:462
  52.4 123.8 %gather_projected.2 = (f32[2048,384]{1,0:T(8,128)}, f32[512,384]{1,0:T(8,128)}) custom-call(f32[512,384]{1,0:T(8,128)} %get-tuple-element.17.part), custom_call_target="tpu_custom_call" | custom-call | tf_op jit(solution)/shard_map/gather_projected/pallas_call | solution.py:450
  176.3 15.6 %update.1 = (f32[2048,512]{1,0:T(8,128)}, f32[512,384]{1,0:T(8,128)}) custom-call(f32[2048,384]{1,0:T(8,128)} %get-tuple-element.16.panel.xr, f32[2048,384]{1,0:T(8,128)} %get-tuple-element.18.yr, f32[512,384]{1,0:T(8,128)} %get-tuple-element.19.xc, f32[512,384]{1,0:T(8,128)} %get-tuple-element.20.yc, f32[2048,512]{1,0:T(8,128)} %omega.3, ...), custom_call_target="tpu_custom_call" | custom-call | tf_op jit(solution)/shard_map/update/pallas_call | solution.py:486
  191.9 124.4 %gather_projected.3 = (f32[2048,384]{1,0:T(8,128)}, f32[512,384]{1,0:T(8,128)}) custom-call(f32[512,384]{1,0:T(8,128)} %get-tuple-element.23.part), custom_call_target="tpu_custom_call" | custom-call | tf_op jit(solution)/shard_map/gather_projected/pallas_call | solution.py:450
  316.2 12.9 %update_last.1 = f32[2048,512]{1,0:T(8,128)} custom-call(f32[2048,384]{1,0:T(8,128)} %get-tuple-element.16.panel.xr, f32[2048,384]{1,0:T(8,128)} %get-tuple-element.24.yr, f32[512,384]{1,0:T(8,128)} %get-tuple-element.19.xc, f32[512,384]{1,0:T(8,128)} %get-tuple-element.25.yc, f32[2048,512]{1,0:T(8,128)} %get-tuple-element.26.omega, ...), custom_call_target="tpu_custom_call" | custom-call | tf_op jit(solution)/shard_map/update_last/pallas_call | solution.py:486

commit v2 on v1

--- a/solution.py
+++ b/solution.py
@@ -212,6 +212,10 @@
 HALVES = 2
 CHUNK = 64 // HALVES
 CHUNKS = 4 * HALVES
+LAGS = (CHUNKS, CHUNKS // 2, 0)
+EARLY_LAG = HALVES
+FAR_LAG = EARLY_LAG + 1
+LOF_LAG = FAR_LAG + 2
 
 
 def gather_projected_kernel(part, panel_out, block, panel, inbox, send, recv, sem):
@@ -243,8 +247,9 @@
     fyh = 1 - yh
 
     def within(h, q):
-        d = (0,) + AROUND
-        return h * 256 + (x + 4 - d[q // HALVES]) % 4 * 64 + q % HALVES * CHUNK
+        n = q // HALVES
+        d = jnp.where(n == 2, 3, jnp.where(n == 3, 2, n))
+        return h * 256 + (x + 4 - d) % 4 * 64 + q % HALVES * CHUNK
 
     def full(base, h, q):
         return panel.at[pl.ds(pl.multiple_of(base + within(h, q), CHUNK), CHUNK)]
@@ -257,7 +262,10 @@
 
     d0 = (z + 8 - x) % 8
     near = jnp.where(jnp.logical_or(d0 <= 2, d0 >= 6), 0, 1)
-    other = 1 - near
+    hops = (d0 + 4 * near) % 8
+    hops = jnp.where(hops > 4, 8 - hops, hops)
+    lag = jnp.where(hops == 0, LAGS[0], jnp.where(hops == 1, LAGS[1], LAGS[2]))
+    mine_lag = jnp.where(near == yh, 0, lag)
     Z = 14
     ZD = Z + 4 * CHUNKS
     FAR = ZD + 4 * CHUNKS
@@ -265,83 +273,154 @@
     LOF = LO + CHUNKS
     CORE = LOF + CHUNKS
 
-    def relay(s, q):
+    def copy(slot, src, dst, to, send_slot=None):
+        return pltpu.make_async_remote_copy(
+            src_ref=src, dst_ref=dst, send_sem=send.at[slot if send_slot is None else send_slot],
+            recv_sem=recv.at[slot], device_id=to, device_id_type=MESH)
+
+    def when(cond, f):
+        pl.when(cond)(f)
+
+    def at(base, h, q):
+        return pl.ds(pl.multiple_of(base + within(h, q), CHUNK), CHUNK)
+
+    def whole_copies(s, q):
         d = (d0 + 4 * s) % 8
         mine = s == yh
-        base = jnp.where(mine, lane, 2048)
-        a, b = full(base, yh, q), early(full(base, fyh, q))
+        ref = full(jnp.where(mine, lane, 2048), yh, q)
+        to = full(lane, yh, q)
         slot = Z + (s * CHUNKS + q) * 2
+        return d, ref, copy(slot, ref, ref, up), [
+            (d <= 3, copy(slot, ref, ref, up)),
+            (jnp.logical_or(d == 0, d >= 6), copy(slot, ref, ref, down, slot + ZD - Z)),
+            (jnp.logical_not(mine), copy(FAR + 2 * q, ref, to, far)),
+            (mine, copy(LO + q, late(to), late(to), lo)),
+            (mine, copy(CORE + q, to, to, core)),
+        ]
+
+    def early_copies(s, q):
+        d = (d0 + 4 * s) % 8
+        mine = s == yh
+        ref = early(full(jnp.where(mine, lane, 2048), fyh, q))
+        to = early(full(lane, fyh, q))
+        slot = Z + (s * CHUNKS + q) * 2 + 1
+        return d, ref, copy(slot, ref, ref, up), [
+            (d <= 2, copy(slot, ref, ref, up)),
+            (jnp.logical_or(d == 0, d >= 5), copy(slot, ref, ref, down, slot + ZD - Z)),
+            (jnp.logical_not(mine), copy(FAR + 2 * q + 1, ref, to, far)),
+        ]
+
+    def relay_whole(s, q):
+        d, ref, arrival, copies = whole_copies(s, q)
 
         @pl.when(d == 0)
         def _():
-            at = pl.ds(pl.multiple_of(within(yh, q), CHUNK), CHUNK)
-            to = pl.ds(pl.multiple_of(base + within(yh, q), CHUNK), CHUNK)
-            panel[to] = block[at]
+            panel[at(jnp.where(s == yh, lane, 2048), yh, q)] = block[at(0, yh, q)]
 
         @pl.when(d != 0)
         def _():
-            cp.make(slot, a, a, up).wait_recv()
-
-        cp.start_if(d <= 3, slot, a, a, up)
-        cp.start_if(jnp.logical_or(d == 0, d >= 6), slot, a, a, down, slot + ZD - Z)
-        la, lb = full(lane, yh, q), early(full(lane, fyh, q))
-        theirs = jnp.logical_not(mine)
-        cp.start_if(theirs, FAR + 2 * q, a, la, far)
-        cp.start_if(mine, LO + q, late(la), late(la), lo)
-        cp.start_if(mine, CORE + q, la, la, core)
+            arrival.wait_recv()
+
+        for cond, c in copies:
+            when(cond, c.start)
+
+    def relay_early(s, q):
+        d, ref, arrival, copies = early_copies(s, q)
 
         @pl.when(d == 0)
         def _():
-            at = pl.ds(pl.multiple_of(within(fyh, q), CHUNK), CHUNK)
-            to = pl.ds(pl.multiple_of(base + within(fyh, q), CHUNK), CHUNK)
-            panel[to, :EARLY] = block[at, :EARLY]
+            panel[at(jnp.where(s == yh, lane, 2048), fyh, q), :EARLY] = block[at(0, fyh, q), :EARLY]
 
         @pl.when(d != 0)
         def _():
-            cp.make(slot + 1, b, b, up).wait_recv()
-
-        cp.start_if(d <= 2, slot + 1, b, b, up)
-        cp.start_if(jnp.logical_or(d == 0, d >= 5), slot + 1, b, b, down, slot + 1 + ZD - Z)
-        cp.start_if(theirs, FAR + 2 * q + 1, b, lb, far)
-
-    def far_in(q):
+            arrival.wait_recv()
+
+        for cond, c in copies:
+            when(cond, c.start)
+
+    def far_copies(q):
         a, b = full(flane, fyh, q), early(full(flane, yh, q))
-        cp.make(FAR + 2 * q, a, a, far).wait_recv()
-        cp.start(LOF + q, late(a), late(a), lo)
-        cp.start(CORE + CHUNKS + q, a, a, core)
-        cp.make(FAR + 2 * q + 1, b, b, far).wait_recv()
-
-    def lo_in(q):
+        return [copy(FAR + 2 * q, a, a, far), copy(FAR + 2 * q + 1, b, b, far)], [
+            copy(LOF + q, late(a), late(a), lo), copy(CORE + CHUNKS + q, a, a, core)]
+
+    def lo_copies(q):
         a = full(flane, yh, q)
-        cp.make(LO + q, late(a), late(a), lo).wait_recv()
-        cp.start(CORE + 2 * CHUNKS + q, a, a, core)
-
-    def lof_in(q):
+        return [copy(LO + q, late(a), late(a), lo)], [copy(CORE + 2 * CHUNKS + q, a, a, core)]
+
+    def lof_copies(q):
         a = full(lane, fyh, q)
-        cp.make(LOF + q, late(a), late(a), lo).wait_recv()
-        cp.start(CORE + 3 * CHUNKS + q, a, a, core)
+        return [copy(LOF + q, late(a), late(a), lo)], [copy(CORE + 3 * CHUNKS + q, a, a, core)]
+
+    def pass_on(copies):
+        arrivals, sends = copies
+        for c in arrivals:
+            c.wait_recv()
+        for c in sends:
+            c.start()
+
+    def ranged(q, f):
+        @pl.when(jnp.logical_and(q >= 0, q < CHUNKS))
+        def _():
+            f(q)
 
     piece = column_piece(block, x, y, 0)
-    column_middle(cp, block, x, y, z, k, COL)
-    for q in range(CHUNKS + 4):
-        if q < CHUNKS:
-            if q % HALVES == 0 and q:
-                d = AROUND[q // HALVES - 1]
-                cp.make(COL + d, piece, piece, core).wait_recv()
-                cp.make(COL + 3 + d, piece, piece, core).wait_recv()
-            relay(near, q)
-        if 2 <= q < CHUNKS + 2:
-            relay(other, q - 2)
-        if 3 <= q < CHUNKS + 3:
-            far_in(q - 3)
-            lo_in(q - 3)
-        if 4 <= q < CHUNKS + 4:
-            lof_in(q - 4)
-    for g in range(4):
-        for q in range(CHUNKS):
-            ref = full(lane, yh, q)
-            cp.make(CORE + g * CHUNKS + q, ref, ref, core).wait_recv()
+    source = hops == 0
+
+    def column_arrival(i):
+        copy(COL + i, piece, piece, core).wait_recv()
+
+    def step(t, _):
+        @pl.when(t == EARLY_LAG)
+        def _():
+            theirs = column_piece(block, x, y, 0, 2)
+            column_arrival(0)
+            for d in AROUND:
+                copy(COL + 3 + d, theirs, theirs, device((x + d) % 4, y, z, k)).start()
+
+        for i, d in enumerate(AROUND):
+            @pl.when(jnp.logical_and(source, t == (i + 1) * HALVES))
+            def _():
+                column_arrival(d)
+
+            @pl.when(jnp.logical_and(source, t == (i + 1) * HALVES + EARLY_LAG))
+            def _():
+                column_arrival(3 + d)
+
+        other = 1 - near
+        ranged(t, lambda q: relay_whole(near, q))
+        ranged(t - EARLY_LAG, lambda q: relay_early(near, q))
+        ranged(t - lag, lambda q: relay_whole(other, q))
+        ranged(t - lag - EARLY_LAG, lambda q: relay_early(other, q))
+        ranged(t - mine_lag - FAR_LAG, lambda q: pass_on(far_copies(q)))
+        ranged(t - mine_lag - FAR_LAG, lambda q: pass_on(lo_copies(q)))
+        ranged(t - mine_lag - LOF_LAG, lambda q: pass_on(lof_copies(q)))
+        return 0
+
+    lax.fori_loop(0, CHUNKS + max(LAGS) + LOF_LAG, step, 0)
+
+    @pl.when(jnp.logical_not(source))
+    def _():
+        for i in range(1, 7):
+            column_arrival(i)
+
+    def end(q, _):
+        for s in (0, 1):
+            for _, _, _, copies in (whole_copies(s, q), early_copies(s, q)):
+                for cond, c in copies:
+                    when(cond, c.wait_send)
+        for arrivals, sends in (far_copies(q), lo_copies(q), lof_copies(q)):
+            for c in sends:
+                c.wait_send()
+        ref = full(lane, yh, q)
+        for g in range(4):
+            copy(CORE + g * CHUNKS + q, ref, ref, core).wait_recv()
+        return 0
+
+    lax.fori_loop(0, CHUNKS, end, 0)
     cp.finish()
+    theirs = column_piece(block, x, y, 0, 2)
+    for d in AROUND:
+        copy(COL + 3 + d, theirs, theirs, core).wait_send()
     out = pltpu.make_async_copy(panel.at[pl.ds(0, 2048)], panel_out, sem)
     out.start()
     out.wait()

time: 331 us -> 202 us (0.61)
  Pallas kernels: 329 us -> 201 us
    pallas_call x2, Pallas kernels: 248 us -> 120 us  [gather_projected(): pl.pallas_call(gather_projected_kernel, out_shape=(shape(2048, S), shape(...]
where the time goes in v2:
time: 202 us; the launch traced here: 201 us
  Pallas kernels  201 us (100%)
    pallas_call x2, Pallas kernels, gather_projected(): pl.pallas_call(gather_projected_kernel, out_shape=(shape(2048, S), shape(...  120 us
    pallas_call x1, Pallas kernels, gather_samples(): pl.pallas_call(gather_samples_kernel, out_shape=(shape(2048, S), shape(51...  42.2 us
    pallas_call x2, Pallas kernels, update(): pl.pallas_call(functools.partial(update_kernel, last, S), grid=(2048 // T...  28.5 us
    pallas_call x1, Pallas kernels, first_partial(): pl.pallas_call(first_partial_kernel, grid=(2048 // TILE,), out_shape=(sha...  10.2 us

profile of v2, /device:TPU:25, one launch (start us, length us, event | category | flops | bytes accessed | tf_op | source)
XLA Modules:
  0.0 201.3 jit_solution(1017348601153040523)
XLA Ops:
  0.0 42.2 %gather_samples.1 = (f32[2048,384]{1,0:T(8,128)}, f32[512,384]{1,0:T(8,128)}) custom-call(f32[64,384]{1,0:T(8,128)} %bitcast.1), custom_call_target="tpu_custom_call" | custom-call | tf_op jit(solution)/shard_map/gather_samples/pallas_call | solution.py:517
  42.2 10.2 %first_partial.1 = (bf16[384,2048]{1,0:T(8,128)(2,1)}, bf16[384,2048]{1,0:T(8,128)(2,1)}, f32[512,384]{1,0:T(8,128)}) custom-call(f32[2048,384]{1,0:T(8,128)} %get-tuple-element.16.panel.xr, f32[2048,512]{1,0:T(8,128)} %omega.3), custom_call_target="tpu_custom_call" | custom-call | tf_op jit(solution)/shard_map/first_partial/pallas_call | solution.py:541
  52.4 59.6 %gather_projected.2 = (f32[2048,384]{1,0:T(8,128)}, f32[512,384]{1,0:T(8,128)}) custom-call(f32[512,384]{1,0:T(8,128)} %get-tuple-element.17.part), custom_call_target="tpu_custom_call" | custom-call | tf_op jit(solution)/shard_map/gather_projected/pallas_call | solution.py:529
  112.1 15.6 %update.1 = (f32[2048,512]{1,0:T(8,128)}, f32[512,384]{1,0:T(8,128)}) custom-call(f32[2048,384]{1,0:T(8,128)} %get-tuple-element.16.panel.xr, f32[2048,384]{1,0:T(8,128)} %get-tuple-element.18.yr, f32[512,384]{1,0:T(8,128)} %get-tuple-element.19.xc, f32[512,384]{1,0:T(8,128)} %get-tuple-element.20.yc, f32[2048,512]{1,0:T(8,128)} %omega.3, ...), custom_call_target="tpu_custom_call" | custom-call | tf_op jit(solution)/shard_map/update/pallas_call | solution.py:565
  127.7 60.8 %gather_projected.3 = (f32[2048,384]{1,0:T(8,128)}, f32[512,384]{1,0:T(8,128)}) custom-call(f32[512,384]{1,0:T(8,128)} %get-tuple-element.23.part), custom_call_target="tpu_custom_call" | custom-call | tf_op jit(solution)/shard_map/gather_projected/pallas_call | solution.py:529
  188.4 12.9 %update_last.1 = f32[2048,512]{1,0:T(8,128)} custom-call(f32[2048,384]{1,0:T(8,128)} %get-tuple-element.16.panel.xr, f32[2048,384]{1,0:T(8,128)} %get-tuple-element.24.yr, f32[512,384]{1,0:T(8,128)} %get-tuple-element.19.xc, f32[512,384]{1,0:T(8,128)} %get-tuple-element.25.yc, f32[2048,512]{1,0:T(8,128)} %get-tuple-element.26.omega, ...), custom_call_target="tpu_custom_call" | custom-call | tf_op jit(solution)/shard_map/update_last/pallas_call | solution.py:565

commit v3 on v2

--- a/solution.py
+++ b/solution.py
@@ -1,5 +1,3 @@
-import functools
-
 import jax
 import jax.numpy as jnp
 from jax import lax
@@ -69,13 +67,6 @@
                     copy.wait_send()
 
 
-def greet(partners):
-    barrier = pltpu.get_barrier_semaphore()
-    for partner in partners:
-        pl.semaphore_signal(barrier, inc=1, device_id=partner, device_id_type=MESH)
-    pl.semaphore_wait(barrier, len(partners))
-
-
 def column_piece(buf, x, y, d, e=0):
     return buf.at[rows((((y + e) % 4) // 2 * 4 + (x + 4 - d) % 4) * 64, 64)]
 
@@ -104,13 +95,44 @@
         cp.make(base + 3 + d, mine, mine, (0, 0)).wait_recv()
 
 
-def gather_samples_kernel(own_ref, panel, block, send, recv, sem):
-    x, y, z, k = place()
+CHUNK = 64
+CHUNKS = 4
+LAGS = (4, 2, 0)
+EARLY_LAG = 1
+FAR_LAG = EARLY_LAG + 1
+LOF_LAG = FAR_LAG + 2
+K3 = 6 * S
+BLOCK = 256
+
+
+def split(a):
+    hi = a.astype(BF16)
+    return hi, (a - hi.astype(F32)).astype(BF16)
+
+
+def partial_block(i, acc, flipped, omega, right):
+    hi, lo = split(omega[rows(i * BLOCK, BLOCK)])
+    right[:BLOCK] = hi
+    right[BLOCK:2 * BLOCK] = lo
+    right[2 * BLOCK:] = hi
+    acc[...] += jnp.dot(flipped[i], right[...], preferred_element_type=F32)
+
+
+def flip_block(i, flipped, panel):
+    hi, lo = split(panel[rows(i * BLOCK, BLOCK)].T)
+    flipped[i, :, :BLOCK] = hi
+    flipped[i, :, BLOCK:2 * BLOCK] = hi
+    flipped[i, :, 2 * BLOCK:] = lo
+
+
+def gather_samples(own_ref, panel, block, send, recv, where, partial):
+    x, y, z, k = where
     yl, yh = y % 2, y // 2
     r, c = yh * 4 + x, z * 4 + yl * 2 + k
     up = device(x, y, (z + 1) % 8, k)
     down = device(x, y, (z + 7) % 8, k)
     lo = device(x, yh * 2 + 1 - yl, z, k)
+    far = device(x, 3 - y, z, k)
     core = device(x, y, z, 1 - k)
     to_r, to_c = c % 8, r * 4 + c // 8
     own_b = c * 8 + r
@@ -120,7 +142,7 @@
     cp = Copies(send, recv)
 
     barrier = pltpu.get_barrier_semaphore()
-    partners = [up, down, lo, core] + group
+    partners = [up, down, lo, far, core] + group
     for partner in partners:
         pl.semaphore_signal(barrier, inc=1, device_id=partner, device_id_type=MESH)
 
@@ -164,7 +186,11 @@
         cp.make(LO + i, late(piece), late(piece), lo).wait_recv()
         cp.start(CORE_LO + i, piece, piece, core)
 
-    n = 1
+    def multiply(i, zz):
+        cp.make(CORE + i, own, own, core).wait_recv()
+        cp.make(CORE_LO + i, own, own, core).wait_recv()
+        partial(zz)
+
     for t in range(1, 5):
         a = at((z + 8 - t) % 8, yl)
         b = at((z + t) % 8, yl)
@@ -201,25 +227,21 @@
         else:
             lo_arrived(2 * t - 3, (z + 8 - (t - 1)) % 8)
             lo_arrived(2 * t - 2, (z + t - 1) % 8)
+        if t == 2:
+            multiply(0, z)
+        if t > 2:
+            multiply(2 * t - 5, (z + 8 - (t - 2)) % 8)
+            multiply(2 * t - 4, (z + t - 2) % 8)
+    multiply(5, (z + 5) % 8)
     lo_arrived(7, (z + 4) % 8)
+    multiply(6, (z + 3) % 8)
+    multiply(7, (z + 4) % 8)
     column_end(cp, block, x, y, z, k, COL)
-    for i in range(8):
-        cp.make(CORE + i, own, own, core).wait_recv()
-        cp.make(CORE_LO + i, own, own, core).wait_recv()
     cp.finish()
 
 
-HALVES = 2
-CHUNK = 64 // HALVES
-CHUNKS = 4 * HALVES
-LAGS = (CHUNKS, CHUNKS // 2, 0)
-EARLY_LAG = HALVES
-FAR_LAG = EARLY_LAG + 1
-LOF_LAG = FAR_LAG + 2
-
-
-def gather_projected_kernel(part, panel_out, block, panel, inbox, send, recv, sem):
-    x, y, z, k = place()
+def gather_projected(acc, part, block, panel, inbox, send, recv, where):
+    x, y, z, k = where
     yl, yh = y % 2, y // 2
     r = yh * 4 + x
     up = device(x, y, (z + 1) % 8, k)
@@ -227,13 +249,20 @@
     lo = device(x, yh * 2 + 1 - yl, z, k)
     far = device(x, 3 - y, z, k)
     core = device(x, y, z, 1 - k)
-    group = [((x + d) % 4, (y + e) % 4) for d in (2, 1, 3, 0) for e in (2, 0) if d or e]
     cp = Copies(send, recv)
-    greet([up, down, lo, far, core] + [device(tx, ty, z, k) for tx, ty in group])
-
-    for i, (tx, ty) in enumerate(group):
-        tr = (ty // 2) * 4 + tx
-        cp.start(i, part.at[rows(tr * 64, 64)], inbox.at[i], device(tx, ty, z, k))
+
+    def scatter_copy(p):
+        slot = (r + 7 - p) % 8
+        return p != r, pltpu.make_async_remote_copy(
+            src_ref=part.at[rows(p * 64, 64)], dst_ref=inbox.at[slot], send_sem=send.at[slot], recv_sem=recv.at[slot],
+            device_id=device(p % 4, p // 4 * 2 + yl, z, k), device_id_type=MESH)
+
+    for i in range(4):
+        j = (r // 2 + 1 + i) % 4
+        part[rows(j * 128, 128)] = acc[:, pl.ds(pl.multiple_of(j * 128, 128), 128)].T
+        for p in (2 * j, 2 * j + 1):
+            cond, c = scatter_copy(p)
+            pl.when(cond)(c.start)
     total = part[rows(r * 64, 64)]
     for i in range(7):
         cp.make(i, inbox.at[i], inbox.at[i], core).wait_recv()
@@ -247,9 +276,8 @@
     fyh = 1 - yh
 
     def within(h, q):
-        n = q // HALVES
-        d = jnp.where(n == 2, 3, jnp.where(n == 3, 2, n))
-        return h * 256 + (x + 4 - d) % 4 * 64 + q % HALVES * CHUNK
+        d = jnp.where(q == 2, 3, jnp.where(q == 3, 2, q))
+        return h * 256 + (x + 4 - d) % 4 * 64
 
     def full(base, h, q):
         return panel.at[pl.ds(pl.multiple_of(base + within(h, q), CHUNK), CHUNK)]
@@ -378,11 +406,11 @@
                 copy(COL + 3 + d, theirs, theirs, device((x + d) % 4, y, z, k)).start()
 
         for i, d in enumerate(AROUND):
-            @pl.when(jnp.logical_and(source, t == (i + 1) * HALVES))
+            @pl.when(jnp.logical_and(source, t == i + 1))
             def _():
                 column_arrival(d)
 
-            @pl.when(jnp.logical_and(source, t == (i + 1) * HALVES + EARLY_LAG))
+            @pl.when(jnp.logical_and(source, t == i + 1 + EARLY_LAG))
             def _():
                 column_arrival(3 + d)
 
@@ -421,167 +449,108 @@
     theirs = column_piece(block, x, y, 0, 2)
     for d in AROUND:
         copy(COL + 3 + d, theirs, theirs, core).wait_send()
-    out = pltpu.make_async_copy(panel.at[pl.ds(0, 2048)], panel_out, sem)
-    out.start()
-    out.wait()
-
-
-def split(a):
-    hi = a.astype(BF16)
-    return hi, (a - hi.astype(F32)).astype(BF16)
-
-
-def dot3(ah, al, bh, bl, dims):
-    d = lambda p, q: lax.dot_general(p, q, (dims, ((), ())), preferred_element_type=F32)
-    return d(ah, bh) + (d(ah, bl) + d(al, bh))
-
-
-TILE = 256
-NN = ((1,), (0,))
-NT = ((1,), (1,))
-
-
-def first_partial_kernel(panel, omega, xh_out, xl_out, part, acc):
-    i = pl.program_id(0)
-    xh, xl = split(panel[...].T)
-    xh_out[...] = xh
-    xl_out[...] = xl
-    oh, ol = split(omega[...])
-
-    @pl.when(i == 0)
+    for p in range(8):
+        cond, c = scatter_copy(p)
+        pl.when(cond)(c.wait_send)
+
+
+TILE = 512
+
+
+def update_tile(i, where, count, samples, projected, omega, left, right):
+    x, y, z, k = where
+    at = rows(i * TILE, TILE)
+    for j, ref in enumerate((samples, projected)):
+        hi, lo = split(ref[at])
+        left[:, j * S:(j + 1) * S] = hi
+        left[:, (j + 2) * S:(j + 3) * S] = hi
+        left[:, (j + 4) * S:(j + 5) * S] = lo
+    cross = lax.dot_general(left[...], right[...], (((1,), (1,)), ((), ())), preferred_element_type=F32)
+    old = omega[at]
+    moved = old - (STEP * 0.5 / count) * cross
+    threshold = STEP * PENALTY
+    new = moved - jnp.clip(moved, -threshold, threshold)
+    omega[at] = new
+
+    @pl.when(((y // 2) * 4 + x) * 4 + i == z * 4 + (y % 2) * 2 + k)
     def _():
-        acc[...] = jnp.zeros_like(acc)
-
-    acc[...] += dot3(xh, xl, oh, ol, NN)
-
-    @pl.when(i == pl.num_programs(0) - 1)
-    def _():
-        part[...] = acc[...].T
-
-
-def update_kernel(last, count, xr, yr, xc, yc, omega, xh, xl, *rest):
-    if last:
-        out, rh, rl = rest
-    else:
-        out, part, rh, rl, acc = rest
-    i = pl.program_id(0)
-    row0 = lax.axis_index("row") * 2048 + i * TILE
-    col0 = lax.axis_index("col") * 512
-
-    @pl.when(i == 0)
-    def _():
-        h, l = split(yc[...])
-        rh[:, :S] = h
-        rl[:, :S] = l
-        h, l = split(xc[...])
-        rh[:, S:] = h
-        rl[:, S:] = l
-        if not last:
-            acc[...] = jnp.zeros_like(acc)
-
-    ah, al = split(jnp.concatenate([xr[...], yr[...]], axis=1))
-    cross = dot3(ah, al, rh[...], rl[...], NT)
-    old = omega[...]
-    moved = old - (STEP * 0.5 / count) * cross
-    thr = STEP * PENALTY
-    new = moved - jnp.clip(moved, -thr, thr)
-    out[...] = new
-
-    @pl.when(jnp.logical_and(row0 < col0 + 512, col0 < row0 + TILE))
-    def _():
-        gr = row0 + lax.broadcasted_iota(jnp.int32, (TILE, 512), 0)
-        gc = col0 + lax.broadcasted_iota(jnp.int32, (TILE, 512), 1)
-        on = gr == gc
+        shape = (TILE, TILE)
+        on = lax.broadcasted_iota(jnp.int32, shape, 0) == lax.broadcasted_iota(jnp.int32, shape, 1)
         safe = jnp.where(on, old, 1.0)
-        out[...] = jnp.where(on, moved + STEP / safe, new)
-
-    if not last:
-        nh, nl = split(out[...])
-        acc[...] += dot3(xh[...], xl[...], nh, nl, NN)
-
-        @pl.when(i == pl.num_programs(0) - 1)
-        def _():
-            part[...] = acc[...].T
-
-
-def shape(*dims, dtype=F32):
-    return jax.ShapeDtypeStruct(dims, dtype)
-
-
-def vm():
-    return pl.BlockSpec(memory_space=pltpu.VMEM)
-
-
-def gather_samples(own):
-    n = 48
+        omega[at] = jnp.where(on, moved + STEP / safe, new)
+
+
+def set_right(right, block, first):
+    hi, lo = split(block[...])
+    right[:, first * S:(first + 1) * S] = hi
+    right[:, (first + 2) * S:(first + 3) * S] = lo
+    right[:, (first + 4) * S:(first + 5) * S] = hi
+
+
+def kernel(own_ref, omega_ref, out_ref, omega, samples, samples_block, flipped, acc, part, projected0, projected1,
+           block0, block1, inbox0, inbox1, left, right, tall, x_send, x_recv, send0, recv0, send1, recv1, in_sem, out_sem):
+    where = place()
+    load = pltpu.make_async_copy(omega_ref, omega, in_sem)
+    load.start()
+    acc[...] = jnp.zeros_like(acc)
+    loaded = []
+
+    def partial(zz):
+        flip_block(zz, flipped, samples)
+        if not loaded:
+            load.wait()
+            loaded.append(True)
+        partial_block(zz, acc, flipped, omega, tall)
+
+    gather_samples(own_ref, samples, samples_block, x_send, x_recv, where, partial)
+    gather_projected(acc, part, block0, projected0, inbox0, send0, recv0, where)
+    set_right(right, samples_block, 1)
+    set_right(right, block0, 0)
+    acc[...] = jnp.zeros_like(acc)
+
+    def first(i, _):
+        update_tile(i, where, S, samples, projected0, omega, left, right)
+        partial_block(2 * i, acc, flipped, omega, tall)
+        partial_block(2 * i + 1, acc, flipped, omega, tall)
+        return 0
+
+    lax.fori_loop(0, 2048 // TILE, first, 0)
+    gather_projected(acc, part, block1, projected1, inbox1, send1, recv1, where)
+    set_right(right, block1, 0)
+
+    def store(i):
+        at = rows(i * TILE, TILE)
+        return pltpu.make_async_copy(omega.at[at], out_ref.at[at], out_sem.at[i])
+
+    def second(i, _):
+        update_tile(i, where, S, samples, projected1, omega, left, right)
+        store(i).start()
+        return 0
+
+    lax.fori_loop(0, 2048 // TILE, second, 0)
+    for i in range(2048 // TILE):
+        store(i).wait()
+
+
+def body(samples, omega):
+    n = 14 + 16 * CHUNKS
+    dma = pltpu.SemaphoreType.DMA
+    vmem = pltpu.VMEM
     return pl.pallas_call(
-        gather_samples_kernel,
-        out_shape=(shape(2048, S), shape(512, S)),
-        in_specs=[vm()], out_specs=(vm(), vm()),
-        scratch_shapes=[pltpu.SemaphoreType.DMA((n,)), pltpu.SemaphoreType.DMA((n,)), pltpu.SemaphoreType.DMA],
+        kernel,
+        out_shape=jax.ShapeDtypeStruct((2048, 512), F32),
+        in_specs=[pl.BlockSpec(memory_space=pltpu.VMEM), pl.BlockSpec(memory_space=pl.ANY)],
+        out_specs=pl.BlockSpec(memory_space=pl.ANY),
+        scratch_shapes=[
+            vmem((2048, 512), F32), vmem((2048, S), F32), vmem((512, S), F32), vmem((8, S, 3 * BLOCK), BF16),
+            vmem((S, 512), F32), vmem((512, S), F32), vmem((2560, S), F32), vmem((2560, S), F32),
+            vmem((512, S), F32), vmem((512, S), F32), vmem((7, 64, S), F32), vmem((7, 64, S), F32),
+            vmem((TILE, K3), BF16), vmem((512, K3), BF16), vmem((3 * BLOCK, 512), BF16),
+            dma((48,)), dma((48,)), dma((n,)), dma((n,)), dma((n,)), dma((n,)), dma, dma((2048 // TILE,)),
+        ],
         compiler_params=pltpu.CompilerParams(collective_id=0, has_side_effects=True, vmem_limit_bytes=VMEM_LIMIT),
-        name="gather_samples",
-    )(own)
-
-
-def gather_projected(part):
-    n = 14 + 16 * CHUNKS
-    return pl.pallas_call(
-        gather_projected_kernel,
-        out_shape=(shape(2048, S), shape(512, S)),
-        in_specs=[vm()], out_specs=(vm(), vm()),
-        scratch_shapes=[pltpu.VMEM((2560, S), F32), pltpu.VMEM((7, 64, S), F32),
-                        pltpu.SemaphoreType.DMA((n,)), pltpu.SemaphoreType.DMA((n,)), pltpu.SemaphoreType.DMA],
-        compiler_params=pltpu.CompilerParams(collective_id=1, has_side_effects=True, vmem_limit_bytes=VMEM_LIMIT),
-        name="gather_projected",
-    )(part)
-
-
-def first_partial(panel, omega):
-    return pl.pallas_call(
-        first_partial_kernel,
-        grid=(2048 // TILE,),
-        out_shape=(shape(S, 2048, dtype=BF16), shape(S, 2048, dtype=BF16), shape(512, S)),
-        in_specs=[pl.BlockSpec((TILE, S), lambda i: (i, 0)), pl.BlockSpec((TILE, 512), lambda i: (i, 0))],
-        out_specs=(pl.BlockSpec((S, TILE), lambda i: (0, i)), pl.BlockSpec((S, TILE), lambda i: (0, i)),
-                   pl.BlockSpec((512, S), lambda i: (0, 0))),
-        scratch_shapes=[pltpu.VMEM((S, 512), F32)],
-        compiler_params=pltpu.CompilerParams(vmem_limit_bytes=VMEM_LIMIT),
-        name="first_partial",
-    )(panel, omega)
-
-
-def update(last, xr, yr, xc, yc, omega, xh, xl):
-    tile = pl.BlockSpec((TILE, S), lambda i: (i, 0))
-    whole = pl.BlockSpec((512, S), lambda i: (0, 0))
-    square = pl.BlockSpec((TILE, 512), lambda i: (i, 0))
-    tall = pl.BlockSpec((S, TILE), lambda i: (0, i))
-    scratch = [pltpu.VMEM((512, 2 * S), BF16), pltpu.VMEM((512, 2 * S), BF16)]
-    if last:
-        out_shape, out_specs = shape(2048, 512), square
-    else:
-        out_shape, out_specs = (shape(2048, 512), shape(512, S)), (square, whole)
-        scratch.append(pltpu.VMEM((S, 512), F32))
-    return pl.pallas_call(
-        functools.partial(update_kernel, last, S),
-        grid=(2048 // TILE,),
-        out_shape=out_shape,
-        in_specs=[tile, tile, whole, whole, square, tall, tall],
-        out_specs=out_specs,
-        scratch_shapes=scratch,
-        compiler_params=pltpu.CompilerParams(vmem_limit_bytes=VMEM_LIMIT),
-        name="update_last" if last else "update",
-    )(xr, yr, xc, yc, omega, xh, xl)
-
-
-def body(samples, omega):
-    own = samples.T
-    xr, xc = gather_samples(own)
-    xh, xl, part = first_partial(xr, omega)
-    yr, yc = gather_projected(part)
-    omega, part = update(False, xr, yr, xc, yc, omega, xh, xl)
-    yr, yc = gather_projected(part)
-    return update(True, xr, yr, xc, yc, omega, xh, xl)
+        name="concord_steps",
+    )(samples.T, omega)
 
 
 def solution(mesh):

time: 202 us -> 167 us (0.83)
  Pallas kernels: 201 us -> 160 us
  local copies, waits for them, and re-layouts: 0 us -> 4.64 us
    pallas_call x6 -> x1, Pallas kernels: 201 us -> 160 us  [body(): pl.pallas_call(kernel, out_shape=jax.ShapeDtypeStruct((2048, 512), F32),...]
    unnamed x0 -> x1, local copies, waits for them, and re-layouts: none -> 4.64 us
where the time goes in v3:
time: 167 us; the launch traced here: 165 us
  Pallas kernels  160 us (96%)
  local copies, waits for them, and re-layouts  4.64 us (3%)
    pallas_call x1, Pallas kernels, body(): pl.pallas_call(kernel, out_shape=jax.ShapeDtypeStruct((2048, 512), F32),...  160 us
    unnamed x1, local copies, waits for them, and re-layouts  4.64 us

profile of v3, /device:TPU:25, one launch (start us, length us, event | category | flops | bytes accessed | tf_op | source)
XLA Modules:
  0.0 165.0 jit_solution(16774662812372854843)
XLA Ops:
  0.0 160.3 %concord_steps.1 = f32[2048,512]{1,0:T(8,128)} custom-call(f32[64,384]{1,0:T(8,128)} %bitcast.1, f32[2048,512]{1,0:T(8,128)} %omega_ref.1), custom_call_target="tpu_custom_call" | custom-call | tf_op jit(solution)/shard_map/concord_steps/pallas_call | solution.py:539
  160.3 4.6 %copy.4 = f32[2048,512]{1,0:T(8,128)} copy(f32[2048,512]{1,0:T(8,128)} %concord_steps.1) | data formatting | bytes 8388608

commit v4 on v3

v4 whole, which is shorter than its diff:
```python
import jax
import jax.numpy as jnp
from jax import lax
from jax.experimental import pallas as pl
from jax.experimental.pallas import tpu as pltpu
from jax.sharding import PartitionSpec as P

ITERS = 2
STEP = 0.01
PENALTY = 0.25
S = 384
EARLY = 128
MESH = pl.DeviceIdType.MESH
F32 = jnp.float32
BF16 = jnp.bfloat16
VMEM_LIMIT = 58 * 2**20


def place():
    r = lax.axis_index("row")
    c = lax.axis_index("col")
    return r % 4, (r // 4) * 2 + (c // 2) % 2, c // 4, c % 2


def device(x, y, z, k):
    return (y // 2) * 4 + x, z * 4 + (y % 2) * 2 + k


def rows(start, size):
    return pl.ds(pl.multiple_of(start, 64), size)


def copy(src, dst, send, recv, to):
    return pltpu.make_async_remote_copy(
        src_ref=src, dst_ref=dst, send_sem=send, recv_sem=recv, device_id=to, device_id_type=MESH)


class Copies:
    def __init__(self, send, recv):
        self.send, self.recv = send, recv

    def make(self, slot, src, dst, to):
        return copy(src, dst, self.send, self.recv.at[slot], to)

    def start(self, slot, src, dst, to):
        self.make(slot, src, dst, to).start()


def column_piece(buf, x, y, d, e=0):
    return buf.at[rows((((y + e) % 4) // 2 * 4 + (x + 4 - d) % 4) * 64, 64)]


AROUND = (1, 3, 2)


def column_start(cp, buf, x, y, z, k, base):
    mine = column_piece(buf, x, y, 0)
    for d in AROUND:
        cp.start(base + d, mine, mine, device((x + d) % 4, y, z, k))
    cp.start(base, mine, mine, device(x, (y + 2) % 4, z, k))


def column_middle(cp, buf, x, y, z, k, base):
    theirs = column_piece(buf, x, y, 0, 2)
    cp.make(base, theirs, theirs, (0, 0)).wait_recv()
    for d in AROUND:
        cp.start(base + 3 + d, theirs, theirs, device((x + d) % 4, y, z, k))


PARTS = 1
CHUNK = 64 // PARTS
CHUNKS = 4 * PARTS
HOP = 1.6
EARLY_LAG = 0.3
K3 = 6 * S
BLOCK = 256


def split(a):
    hi = a.astype(BF16)
    return hi, (a - hi.astype(F32)).astype(BF16)


def partial_block(i, acc, flipped, omega, right):
    hi, lo = split(omega[rows(i * BLOCK, BLOCK)])
    right[:BLOCK] = hi
    right[BLOCK:2 * BLOCK] = lo
    right[2 * BLOCK:] = hi
    acc[...] += jnp.dot(flipped[i], right[...], preferred_element_type=F32)


def flip_block(i, flipped, panel):
    hi, lo = split(panel[rows(i * BLOCK, BLOCK)].T)
    flipped[i, :, :BLOCK] = hi
    flipped[i, :, BLOCK:2 * BLOCK] = hi
    flipped[i, :, 2 * BLOCK:] = lo


def gather_samples(own_ref, panel, block, measure, send, recv, where, partial):
    x, y, z, k = where
    yl, yh = y % 2, y // 2
    r, c = yh * 4 + x, z * 4 + yl * 2 + k
    up = device(x, y, (z + 1) % 8, k)
    down = device(x, y, (z + 7) % 8, k)
    lo = device(x, yh * 2 + 1 - yl, z, k)
    far = device(x, 3 - y, z, k)
    core = device(x, y, z, 1 - k)
    to_r, to_c = c % 8, r * 4 + c // 8
    own_b = c * 8 + r
    from_r, from_c = own_b // 32, own_b % 32
    moves = (to_r * 32 + to_c) != (r * 32 + c)
    group = [device((x + d) % 4, (y + e) % 4, z, k) for d in range(4) for e in (0, 2) if d or e]
    cp = Copies(send.at[0], recv)

    barrier = pltpu.get_barrier_semaphore()
    partners = [up, down, lo, far, core] + group
    for partner in partners:
        pl.semaphore_signal(barrier, inc=1, device_id=partner, device_id_type=MESH)

    @pl.when(moves)
    def _():
        pl.semaphore_signal(barrier, inc=1, device_id=(from_r, from_c), device_id_type=MESH)

    def at(zz, l):
        return panel.at[rows((zz * 4 + l * 2 + k) * 64, 64)]

    def early(ref):
        return ref.at[:, pl.ds(0, EARLY)]

    def late(ref):
        return ref.at[:, pl.ds(EARLY, S - EARLY)]

    def half(ref, h):
        return ref.at[pl.ds(h * 32, 32)]

    panel[rows(c * 64, 64)] = own_ref[...]
    pl.semaphore_wait(barrier, len(partners) + jnp.where(moves, 1, 0))

    own = at(z, yl)
    E_OWN, UP, DOWN, UP_E, DOWN_E, LO, CORE, CORE_LO, COL = 0, 48, 56, 8, 12, 16, 24, 32, 40
    PERM = 47
    cp.start(E_OWN, early(own), early(own), lo)
    for h in (0, 1):
        cp.start(UP + h, half(own, h), half(own, h), up)
        cp.start(DOWN + h, half(own, h), half(own, h), down)
    permuted = copy(own, block.at[rows(to_r * 64, 64)], send.at[1], recv.at[PERM], (to_r, to_c))
    pl.when(moves)(permuted.start)

    @pl.when(jnp.logical_not(moves))
    def _():
        block[rows(r * 64, 64)] = own_ref[...]

    cp.start(LO, late(own), late(own), lo)
    cp.start(CORE, own, own, core)
    cp.make(E_OWN, early(own), early(own), lo).wait_recv()
    e = early(at(z, 1 - yl))
    cp.start(UP_E, e, e, up)
    cp.start(DOWN_E, e, e, down)

    def lo_arrived(i, zz):
        piece = at(zz, 1 - yl)
        cp.make(LO + i, late(piece), late(piece), lo).wait_recv()
        cp.start(CORE_LO + i, piece, piece, core)

    def relay(slot, ref, to, more):
        for h in (0, 1):
            part = half(ref, h)
            cp.make(slot + h, part, part, to).wait_recv()
            if more:
                cp.start(slot + 2 + h, part, part, to)

    def multiply(i, zz):
        cp.make(CORE + i, own, own, core).wait_recv()
        cp.make(CORE_LO + i, own, own, core).wait_recv()
        partial(zz)

    for t in range(1, 5):
        a = at((z + 8 - t) % 8, yl)
        b = at((z + t) % 8, yl)
        relay(UP + 2 * t - 2, a, up, t < 4)
        if t < 4:
            relay(DOWN + 2 * t - 2, b, down, t < 3)
        ea = early(at((z + 8 - t) % 8, 1 - yl))
        eb = early(at((z + t) % 8, 1 - yl))
        if t < 4:
            cp.make(UP_E + t - 1, ea, ea, up).wait_recv()
            if t < 3:
                cp.start(UP_E + t, ea, ea, up)
        cp.make(DOWN_E + t - 1, eb, eb, down).wait_recv()
        if t < 4:
            cp.start(DOWN_E + t, eb, eb, down)
        cp.start(LO + 2 * t - 1, late(a), late(a), lo)
        cp.start(CORE + 2 * t - 1, a, a, core)
        if t < 4:
            cp.start(LO + 2 * t, late(b), late(b), lo)
            cp.start(CORE + 2 * t, b, b, core)
        if t == 2:
            @pl.when(moves)
            def _():
                cp.make(PERM, own, own, lo).wait_recv()

            column_start(cp, block, x, y, z, k, COL)
        if t == 3:
            column_middle(cp, block, x, y, z, k, COL)
        if t == 1:
            lo_arrived(0, z)
        else:
            lo_arrived(2 * t - 3, (z + 8 - (t - 1)) % 8)
            lo_arrived(2 * t - 2, (z + t - 1) % 8)
        if t == 2:
            multiply(0, z)
        if t > 2:
            multiply(2 * t - 5, (z + 8 - (t - 2)) % 8)
            multiply(2 * t - 4, (z + t - 2) % 8)
    lo_arrived(7, (z + 4) % 8)
    multiply(5, (z + 5) % 8)
    multiply(6, (z + 3) % 8)
    multiply(7, (z + 4) % 8)
    for i in range(1, 7):
        cp.make(COL + i, own, own, core).wait_recv()

    def finish():
        sent = measure.at[pl.ds(0, 38 * 64)]
        cp.make(0, sent, sent, core).wait_send()
        pl.when(moves)(permuted.wait_send)

    return finish


def timetable(hops, near_is_mine):
    base = {"near": HOP * hops, "other": HOP * (4 - hops)}
    mine = base["near" if near_is_mine else "other"]
    events = [(1.5 * PARTS, 7, "column start", 0), (3.5 * PARTS, 7, "column middle", 0)]
    for q in range(CHUNKS):
        for n, stream in enumerate(("near", "other")):
            events.append((base[stream] + q, 1 + n, stream + " whole", q))
            events.append((base[stream] + q + EARLY_LAG, 1 + n, stream + " early", q))
        events.append((mine + q + HOP, 3, "far whole", q))
        events.append((mine + q + EARLY_LAG + HOP, 4, "far early", q))
        events.append((mine + q + EARLY_LAG + 0.1 + HOP, 5, "lo", q))
        events.append((mine + q + max(2 * HOP, EARLY_LAG + 0.1), 6, "lo far", q))
    return [(name, q) for _, _, name, q in sorted(events)]


RS, CORE, COL, Z, FAR, LO, LOF = 0, 1, 2, 9, 9 + 4 * CHUNKS, 9 + 6 * CHUNKS, 9 + 7 * CHUNKS
FED = 9 + 8 * CHUNKS
RECVS = FED + 4
S_RS, S_CORE, S_COL, S_NEAR, S_SOURCE, S_OTHER, S_FAR, S_LO, S_FED = 0, 1, 2, 3, 5, 7, 9, 11, 12
SENDS = 13


def gather_projected(acc, part, block, panel, inbox, fed, send, recv, where, meanwhile):
    x, y, z, k = where
    yl, yh = y % 2, y // 2
    r = yh * 4 + x
    up = device(x, y, (z + 1) % 8, k)
    down = device(x, y, (z + 7) % 8, k)
    lo = device(x, yh * 2 + 1 - yl, z, k)
    far = device(x, 3 - y, z, k)
    core = device(x, y, z, 1 - k)

    for i in range(4):
        j = (r // 2 + 1 + i) % 4
        part[rows(j * 128, 128)] = acc[:, pl.ds(pl.multiple_of(j * 128, 128), 128)].T
        for p in (2 * j, 2 * j + 1):
            c = copy(part.at[rows(p * 64, 64)], inbox.at[rows((r + 7 - p) % 8 * 64, 64)], send.at[S_RS], recv.at[RS],
                     device(p % 4, p // 4 * 2 + yl, z, k))
            pl.when(p != r)(c.start)
    meanwhile()
    copy(inbox, inbox, send.at[S_RS], recv.at[RS], core).wait_recv()
    total = part[rows(r * 64, 64)]
    for i in range(7):
        total = total + inbox[i * 64:(i + 1) * 64]
    block[rows(r * 64, 64)] = total
    column = Copies(send.at[S_COL], recv)
    piece = column_piece(block, x, y, 0)

    def column_arrival(i):
        column.make(COL + i, piece, piece, core).wait_recv()

    xs = z % 4
    to_source = copy(piece, piece, send.at[S_COL], recv.at[COL + (xs + 4 - x) % 4], device(xs, y, z, k))
    pl.when(x != xs)(to_source.start)
    extra = copy(piece.at[:, pl.ds(0, EARLY)], fed.at[rows(x * 64, 64)], send.at[S_FED], recv.at[FED + x],
                 device(xs, (y + 2) % 4, z, k))
    extra.start()

    def fed_arrival(d):
        at = (x + 4 - d) % 4
        ref = fed.at[rows(at * 64, 64)]
        copy(ref, ref, send.at[S_FED], recv.at[FED + at], core).wait_recv()

    def column_start():
        for d in AROUND:
            c = column.make(COL + d, piece, piece, device((x + d) % 4, y, z, k))
            pl.when((x + d) % 4 != xs)(c.start)
        column.start(COL, piece, piece, device(x, (y + 2) % 4, z, k))

    lane = (yl * 2 + k) * 512
    flane = ((1 - yl) * 2 + k) * 512
    fyh = 1 - yh
    around = [(x + 4 - d) % 4 * 64 + i * CHUNK for d in (0,) + AROUND for i in range(PARTS)]
    within = {"own": [yh * 256 + a for a in around], "far": [fyh * 256 + a for a in around]}

    def chunk(base, half, q):
        return pl.ds(pl.multiple_of(base + within[half][q], CHUNK), CHUNK)

    def whole(base, half, q):
        return panel.at[chunk(base, half, q)]

    def early(ref):
        return ref.at[:, pl.ds(0, EARLY)]

    def late(ref):
        return ref.at[:, pl.ds(EARLY, S - EARLY)]

    d0 = (z + 8 - x) % 8
    near = jnp.where(jnp.logical_or(d0 <= 2, d0 >= 6), 0, 1)
    d = (d0 + 4 * near) % 8
    rising = d <= 2
    on = tuple(jnp.where(rising, a, b) for a, b in zip(up, down))
    back = tuple(jnp.where(rising, b, a) for a, b in zip(up, down))
    hops = jnp.where(rising, d, 8 - d)
    near_is_mine = near == yh

    def run(h, near_mine):
        def relay(stream, kind, q):
            n = 0 if kind == "whole" else 1
            mine = (stream == "near") == near_mine
            base = lane if mine else 2048
            half = "own" if kind == "whole" else "far"
            cut = (lambda ref: ref) if kind == "whole" else early
            ref = cut(whole(base, half, q))
            slot = recv.at[Z + ((0 if mine else 1) * CHUNKS + q) * 2 + n]
            source = stream == "near" and h == 0
            if source:
                dist = ((0,) + AROUND)[q // PARTS]
                if kind == "whole":
                    if q and q % PARTS == 0:
                        column_arrival(dist)
                    panel[chunk(base, half, q)] = block[chunk(0, half, q)]
                else:
                    if q % PARTS == 0:
                        fed_arrival(dist)
                    at = pl.ds(pl.multiple_of(around[q], CHUNK), CHUNK)
                    panel[chunk(base, half, q), :EARLY] = fed[at]
                copy(ref, ref, send.at[S_SOURCE + n], slot, down).start()
            else:
                copy(ref, ref, send.at[S_NEAR], slot, core).wait_recv()
            if stream == "near":
                copy(ref, ref, send.at[S_NEAR + n], slot, on).start()
            elif h > 0:
                c = copy(ref, ref, send.at[S_OTHER + n], slot, back)
                if h == 2:
                    c.start()
                else:
                    pl.when(jnp.logical_not(rising) if kind == "whole" else rising)(c.start)
            if not mine:
                copy(ref, cut(whole(lane, half, q)), send.at[S_FAR + n], recv.at[FAR + 2 * q + n], far).start()
            elif kind == "whole":
                copy(late(ref), late(ref), send.at[S_LO], recv.at[LO + q], lo).start()
                copy(ref, ref, send.at[S_CORE], recv.at[CORE], core).start()

        def arrive(ref, slot):
            copy(ref, ref, send.at[S_CORE], recv.at[slot], core).wait_recv()

        def to_core(ref):
            copy(ref, ref, send.at[S_CORE], recv.at[CORE], core).start()

        for name, q in timetable(h, near_mine):
            if name == "column start":
                column_start()
            elif name == "column middle":
                column_middle(column, block, x, y, z, k, COL)
            elif name == "far whole":
                ref = whole(flane, "far", q)
                arrive(ref, FAR + 2 * q)
                copy(late(ref), late(ref), send.at[S_LO], recv.at[LOF + q], lo).start()
                to_core(ref)
            elif name == "far early":
                arrive(early(whole(flane, "own", q)), FAR + 2 * q + 1)
            elif name == "lo":
                ref = whole(flane, "own", q)
                arrive(late(ref), LO + q)
                to_core(ref)
            elif name == "lo far":
                ref = whole(lane, "far", q)
                arrive(late(ref), LOF + q)
                to_core(ref)
            else:
                relay(*name.split(), q)
        for i in range(1 if h else 4, 7):
            column_arrival(i)

    for h in (0, 1, 2):
        for near_mine in (True, False):
            pl.when(jnp.logical_and(hops == h, near_is_mine if near_mine else jnp.logical_not(near_is_mine)))(
                lambda h=h, near_mine=near_mine: run(h, near_mine))

    def sized(n, columns=S):
        return panel.at[pl.ds(0, n), pl.ds(0, columns)]

    got = sized(1024)
    copy(got, got, send.at[S_CORE], recv.at[CORE], core).wait_recv()

    def finish():
        def sent(slot, ref, cond=None):
            c = copy(ref, ref, send.at[slot], recv.at[RS], core)
            if cond is None:
                c.wait_send()
            else:
                pl.when(cond)(c.wait_send)

        sent(S_RS, sized(448))
        sent(S_COL, sized(448))
        sent(S_CORE, got)
        sent(S_LO, sized(512, S - EARLY))
        sent(S_FED, sized(64, EARLY))
        for n, ref in enumerate((sized(256), sized(256, EARLY))):
            sent(S_NEAR + n, ref)
            sent(S_FAR + n, ref)
            sent(S_SOURCE + n, ref, hops == 0)
            sent(S_OTHER + n, ref, jnp.logical_or(hops == 2, jnp.logical_and(
                hops == 1, rising if n else jnp.logical_not(rising))))

    return finish


TILE = 512


def update_tile(i, where, count, samples, projected, omega, left, right):
    x, y, z, k = where
    at = rows(i * TILE, TILE)
    for j, ref in enumerate((samples, projected)):
        hi, lo = split(ref[at])
        left[:, j * S:(j + 1) * S] = hi
        left[:, (j + 2) * S:(j + 3) * S] = hi
        left[:, (j + 4) * S:(j + 5) * S] = lo
    cross = lax.dot_general(left[...], right[...], (((1,), (1,)), ((), ())), preferred_element_type=F32)
    old = omega[at]
    moved = old - (STEP * 0.5 / count) * cross
    threshold = STEP * PENALTY
    new = moved - jnp.clip(moved, -threshold, threshold)
    omega[at] = new

    @pl.when(((y // 2) * 4 + x) * 4 + i == z * 4 + (y % 2) * 2 + k)
    def _():
        shape = (TILE, TILE)
        on = lax.broadcasted_iota(jnp.int32, shape, 0) == lax.broadcasted_iota(jnp.int32, shape, 1)
        safe = jnp.where(on, old, 1.0)
        omega[at] = jnp.where(on, moved + STEP / safe, new)


def set_right(right, block, first):
    hi, lo = split(block[...])
    right[:, first * S:(first + 1) * S] = hi
    right[:, (first + 2) * S:(first + 3) * S] = lo
    right[:, (first + 4) * S:(first + 5) * S] = hi


def kernel(own_ref, omega_ref, omega, samples, samples_block, flipped, acc, part, part1, projected0, projected1,
           block0, block1, inbox0, inbox1, fed0, fed1, left, right, tall, x_send, x_recv, send0, recv0, send1, recv1, in_sem):
    where = place()
    load = pltpu.make_async_copy(omega_ref, omega, in_sem)
    load.start()
    acc[...] = jnp.zeros_like(acc)
    loaded = []

    def partial(zz):
        flip_block(zz, flipped, samples)
        if not loaded:
            load.wait()
            loaded.append(True)
        partial_block(zz, acc, flipped, omega, tall)

    finish = gather_samples(own_ref, samples, samples_block, projected0, x_send, x_recv, where, partial)
    finish = gather_projected(acc, part, block0, projected0, inbox0, fed0, send0, recv0, where, finish)
    set_right(right, samples_block, 1)
    set_right(right, block0, 0)
    acc[...] = jnp.zeros_like(acc)

    def first(i, _):
        update_tile(i, where, S, samples, projected0, omega, left, right)
        partial_block(2 * i, acc, flipped, omega, tall)
        partial_block(2 * i + 1, acc, flipped, omega, tall)
        return 0

    lax.fori_loop(0, 2048 // TILE, first, 0)
    finish = gather_projected(acc, part1, block1, projected1, inbox1, fed1, send1, recv1, where, finish)
    set_right(right, block1, 0)

    def second(i, _):
        update_tile(i, where, S, samples, projected1, omega, left, right)
        return 0

    lax.fori_loop(0, 2048 // TILE, second, 0)
    finish()


def body(samples, omega):
    dma = pltpu.SemaphoreType.DMA
    vmem = pltpu.VMEM
    return pl.pallas_call(
        kernel,
        out_shape=pltpu.VMEM((2048, 512), F32),
        in_specs=[pl.BlockSpec(memory_space=pltpu.VMEM), pl.BlockSpec(memory_space=pltpu.HBM)],
        out_specs=pl.BlockSpec(memory_space=pltpu.VMEM),
        scratch_shapes=[
            vmem((2048, S), F32), vmem((512, S), F32), vmem((8, S, 3 * BLOCK), BF16),
            vmem((S, 512), F32), vmem((512, S), F32), vmem((512, S), F32), vmem((2560, S), F32), vmem((2560, S), F32),
            vmem((512, S), F32), vmem((512, S), F32), vmem((7 * 64, S), F32), vmem((7 * 64, S), F32), vmem((256, EARLY), F32), vmem((256, EARLY), F32),
            vmem((TILE, K3), BF16), vmem((512, K3), BF16), vmem((3 * BLOCK, 512), BF16),
            dma((2,)), dma((62,)), dma((SENDS,)), dma((RECVS,)), dma((SENDS,)), dma((RECVS,)), dma,
        ],
        compiler_params=pltpu.CompilerParams(collective_id=0, has_side_effects=True, vmem_limit_bytes=VMEM_LIMIT),
        name="concord_steps",
    )(samples.T, omega)


def solution(mesh):
    in_specs = (P(None, ("row", "col")), P("row", "col"))
    out_specs = P("row", "col")
    return jax.shard_map(body, mesh=mesh, in_specs=in_specs, out_specs=out_specs, check_vma=False)
```

time: 167 us -> 158 us (0.946); the launches traced: 165 us -> 158 us
  Pallas kernels: 160 us -> 156 us
  local copies, waits for them, and re-layouts: 4.64 us -> 2.02 us
    pallas_call x1, Pallas kernels: 160 us -> 156 us  [body(): pl.pallas_call(kernel, out_shape=pltpu.VMEM((2048, 512), F32), in_specs=[...]
    unnamed x1, local copies, waits for them, and re-layouts: 4.64 us -> 2.02 us
where the time goes in v4:
time: 158 us
  Pallas kernels  156 us (99%)
  local copies, waits for them, and re-layouts  2.02 us (1%)
    pallas_call x1, Pallas kernels, body(): pl.pallas_call(kernel, out_shape=pltpu.VMEM((2048, 512), F32), in_specs=[...  156 us

profile of v4, /device:TPU:25, one launch (start us, length us, event | category | flops | bytes accessed | tf_op | source)
XLA Modules:
  0.0 158.2 jit_solution(2816294340188475593)
XLA Ops:
  0.0 156.2 %concord_steps.1 = f32[2048,512]{1,0:T(8,128)S(1)} custom-call(f32[64,384]{1,0:T(8,128)} %bitcast.1, f32[2048,512]{1,0:T(8,128)} %omega_ref.1), custom_call_target="tpu_custom_call" | custom-call | tf_op jit(solution)/shard_map/concord_steps/pallas_call | solution.py:504
  156.2 2.0 %copy.4 = f32[2048,512]{1,0:T(8,128)} copy(f32[2048,512]{1,0:T(8,128)S(1)} %concord_steps.1) | data formatting | bytes 8388608

commit v5 on v4

--- a/solution.py
+++ b/solution.py
@@ -67,11 +67,10 @@
         cp.start(base + 3 + d, theirs, theirs, device((x + d) % 4, y, z, k))
 
 
-PARTS = 1
-CHUNK = 64 // PARTS
-CHUNKS = 4 * PARTS
-HOP = 1.6
-EARLY_LAG = 0.3
+CHUNK = 64
+CHUNKS = 4
+HOP = 2.1
+LATE = 4.0
 K3 = 6 * S
 BLOCK = 256
 
@@ -230,21 +229,22 @@
 def timetable(hops, near_is_mine):
     base = {"near": HOP * hops, "other": HOP * (4 - hops)}
     mine = base["near" if near_is_mine else "other"]
-    events = [(1.5 * PARTS, 7, "column start", 0), (3.5 * PARTS, 7, "column middle", 0)]
+    events = [(LATE - 0.1, 0, "late sum", 0), (LATE + 2.0, 7, "column start", 0), (LATE + 5.0, 7, "column middle", 0)]
     for q in range(CHUNKS):
         for n, stream in enumerate(("near", "other")):
-            events.append((base[stream] + q, 1 + n, stream + " whole", q))
-            events.append((base[stream] + q + EARLY_LAG, 1 + n, stream + " early", q))
-        events.append((mine + q + HOP, 3, "far whole", q))
-        events.append((mine + q + EARLY_LAG + HOP, 4, "far early", q))
-        events.append((mine + q + EARLY_LAG + 0.1 + HOP, 5, "lo", q))
-        events.append((mine + q + max(2 * HOP, EARLY_LAG + 0.1), 6, "lo far", q))
+            events.append((base[stream] + q, 1 + n, stream + " early", q))
+            events.append((LATE + base[stream] + q, 1 + n, stream + " whole", q))
+        events.append((mine + q + HOP, 4, "far early", q))
+        events.append((LATE + mine + q + HOP, 3, "far whole", q))
+        events.append((LATE + mine + q + HOP + 0.1, 5, "lo", q))
+        events.append((LATE + mine + q + 2 * HOP, 6, "lo far", q))
     return [(name, q) for _, _, name, q in sorted(events)]
 
 
 RS, CORE, COL, Z, FAR, LO, LOF = 0, 1, 2, 9, 9 + 4 * CHUNKS, 9 + 6 * CHUNKS, 9 + 7 * CHUNKS
 FED = 9 + 8 * CHUNKS
-RECVS = FED + 4
+FEED, RS_EARLY = FED + 4, FED + 8
+RECVS = FED + 9
 S_RS, S_CORE, S_COL, S_NEAR, S_SOURCE, S_OTHER, S_FAR, S_LO, S_FED = 0, 1, 2, 3, 5, 7, 9, 11, 12
 SENDS = 13
 
@@ -259,36 +259,54 @@
     far = device(x, 3 - y, z, k)
     core = device(x, y, z, 1 - k)
 
-    for i in range(4):
-        j = (r // 2 + 1 + i) % 4
-        part[rows(j * 128, 128)] = acc[:, pl.ds(pl.multiple_of(j * 128, 128), 128)].T
-        for p in (2 * j, 2 * j + 1):
-            c = copy(part.at[rows(p * 64, 64)], inbox.at[rows((r + 7 - p) % 8 * 64, 64)], send.at[S_RS], recv.at[RS],
-                     device(p % 4, p // 4 * 2 + yl, z, k))
-            pl.when(p != r)(c.start)
+    def early(ref):
+        return ref.at[:, pl.ds(0, EARLY)]
+
+    def late(ref):
+        return ref.at[:, pl.ds(EARLY, S - EARLY)]
+
+    def scatter(cut, slot):
+        for i in range(1, 8):
+            p = (r + i) % 8
+            copy(cut(part.at[rows(p * 64, 64)]), cut(inbox.at[pl.ds((7 - i) * 64, 64)]), send.at[S_RS], recv.at[slot],
+                 device(p % 4, p // 4 * 2 + yl, z, k)).start()
+
+    part[:, :EARLY] = acc[:EARLY, :].T
+    scatter(early, RS_EARLY)
+    part[:, EARLY:] = acc[EARLY:, :].T
+    scatter(late, RS)
     meanwhile()
-    copy(inbox, inbox, send.at[S_RS], recv.at[RS], core).wait_recv()
-    total = part[rows(r * 64, 64)]
+    own_rows = rows(r * 64, 64)
+    piece = column_piece(block, x, y, 0)
+    column = Copies(send.at[S_COL], recv)
+    copy(early(inbox), early(inbox), send.at[S_RS], recv.at[RS_EARLY], core).wait_recv()
+    total = part[own_rows, :EARLY]
     for i in range(7):
-        total = total + inbox[i * 64:(i + 1) * 64]
-    block[rows(r * 64, 64)] = total
-    column = Copies(send.at[S_COL], recv)
-    piece = column_piece(block, x, y, 0)
+        total = total + inbox[i * 64:(i + 1) * 64, :EARLY]
+    block[own_rows, :EARLY] = total
+    xs = z % 4
+    feed = copy(early(piece), early(piece), send.at[S_COL], recv.at[FEED + x], device(xs, y, z, k))
+    pl.when(x != xs)(feed.start)
+    copy(early(piece), fed.at[rows(x * 64, 64)], send.at[S_FED], recv.at[FED + x], device(xs, (y + 2) % 4, z, k)).start()
+
+    def late_sum():
+        copy(late(inbox), late(inbox), send.at[S_RS], recv.at[RS], core).wait_recv()
+        total = part[own_rows, EARLY:]
+        for i in range(7):
+            total = total + inbox[i * 64:(i + 1) * 64, EARLY:]
+        block[own_rows, EARLY:] = total
+        to_source = copy(late(piece), late(piece), send.at[S_COL], recv.at[COL + (xs + 4 - x) % 4], device(xs, y, z, k))
+        pl.when(x != xs)(to_source.start)
 
     def column_arrival(i):
         column.make(COL + i, piece, piece, core).wait_recv()
-
-    xs = z % 4
-    to_source = copy(piece, piece, send.at[S_COL], recv.at[COL + (xs + 4 - x) % 4], device(xs, y, z, k))
-    pl.when(x != xs)(to_source.start)
-    extra = copy(piece.at[:, pl.ds(0, EARLY)], fed.at[rows(x * 64, 64)], send.at[S_FED], recv.at[FED + x],
-                 device(xs, (y + 2) % 4, z, k))
-    extra.start()
 
     def fed_arrival(d):
         at = (x + 4 - d) % 4
         ref = fed.at[rows(at * 64, 64)]
         copy(ref, ref, send.at[S_FED], recv.at[FED + at], core).wait_recv()
+        if d:
+            copy(ref, ref, send.at[S_FED], recv.at[FEED + at], core).wait_recv()
 
     def column_start():
         for d in AROUND:
@@ -299,7 +317,7 @@
     lane = (yl * 2 + k) * 512
     flane = ((1 - yl) * 2 + k) * 512
     fyh = 1 - yh
-    around = [(x + 4 - d) % 4 * 64 + i * CHUNK for d in (0,) + AROUND for i in range(PARTS)]
+    around = [(x + 4 - d) % 4 * 64 for d in (0,) + AROUND]
     within = {"own": [yh * 256 + a for a in around], "far": [fyh * 256 + a for a in around]}
 
     def chunk(base, half, q):
@@ -307,12 +325,6 @@
 
     def whole(base, half, q):
         return panel.at[chunk(base, half, q)]
-
-    def early(ref):
-        return ref.at[:, pl.ds(0, EARLY)]
-
-    def late(ref):
-        return ref.at[:, pl.ds(EARLY, S - EARLY)]
 
     d0 = (z + 8 - x) % 8
     near = jnp.where(jnp.logical_or(d0 <= 2, d0 >= 6), 0, 1)
@@ -328,38 +340,39 @@
             n = 0 if kind == "whole" else 1
             mine = (stream == "near") == near_mine
             base = lane if mine else 2048
-            half = "own" if kind == "whole" else "far"
-            cut = (lambda ref: ref) if kind == "whole" else early
-            ref = cut(whole(base, half, q))
+            cut, halves = (early, ("own", "far")) if n else (late, ("own",))
+            refs = [cut(whole(base, half, q)) for half in halves]
             slot = recv.at[Z + ((0 if mine else 1) * CHUNKS + q) * 2 + n]
             source = stream == "near" and h == 0
             if source:
-                dist = ((0,) + AROUND)[q // PARTS]
-                if kind == "whole":
-                    if q and q % PARTS == 0:
-                        column_arrival(dist)
-                    panel[chunk(base, half, q)] = block[chunk(0, half, q)]
+                dist = ((0,) + AROUND)[q]
+                if n:
+                    fed_arrival(dist)
+                    panel[chunk(base, "own", q), :EARLY] = block[chunk(0, "own", q), :EARLY]
+                    panel[chunk(base, "far", q), :EARLY] = fed[rows(around[q], 64)]
                 else:
-                    if q % PARTS == 0:
-                        fed_arrival(dist)
-                    at = pl.ds(pl.multiple_of(around[q], CHUNK), CHUNK)
-                    panel[chunk(base, half, q), :EARLY] = fed[at]
-                copy(ref, ref, send.at[S_SOURCE + n], slot, down).start()
+                    if q:
+                        copy(late(piece), late(piece), send.at[S_COL], recv.at[COL + dist], core).wait_recv()
+                    panel[chunk(base, "own", q), EARLY:] = block[chunk(0, "own", q), EARLY:]
             else:
-                copy(ref, ref, send.at[S_NEAR], slot, core).wait_recv()
-            if stream == "near":
-                copy(ref, ref, send.at[S_NEAR + n], slot, on).start()
-            elif h > 0:
-                c = copy(ref, ref, send.at[S_OTHER + n], slot, back)
-                if h == 2:
-                    c.start()
-                else:
-                    pl.when(jnp.logical_not(rising) if kind == "whole" else rising)(c.start)
-            if not mine:
-                copy(ref, cut(whole(lane, half, q)), send.at[S_FAR + n], recv.at[FAR + 2 * q + n], far).start()
-            elif kind == "whole":
-                copy(late(ref), late(ref), send.at[S_LO], recv.at[LO + q], lo).start()
-                copy(ref, ref, send.at[S_CORE], recv.at[CORE], core).start()
+                both = panel.at[pl.ds(0, 128), pl.ds(0, EARLY)] if n else refs[0]
+                copy(both, both, send.at[S_NEAR], slot, core).wait_recv()
+            for ref, half in zip(refs, halves):
+                if source:
+                    copy(ref, ref, send.at[S_SOURCE + n], slot, down).start()
+                if stream == "near":
+                    copy(ref, ref, send.at[S_NEAR + n], slot, on).start()
+                elif h > 0:
+                    c = copy(ref, ref, send.at[S_OTHER + n], slot, back)
+                    if h == 2:
+                        c.start()
+                    else:
+                        pl.when(rising if n else jnp.logical_not(rising))(c.start)
+                if not mine:
+                    copy(ref, cut(whole(lane, half, q)), send.at[S_FAR + n], recv.at[FAR + 2 * q + n], far).start()
+            if mine and not n:
+                copy(refs[0], refs[0], send.at[S_LO], recv.at[LO + q], lo).start()
+                to_core(whole(lane, "own", q))
 
         def arrive(ref, slot):
             copy(ref, ref, send.at[S_CORE], recv.at[slot], core).wait_recv()
@@ -368,17 +381,19 @@
             copy(ref, ref, send.at[S_CORE], recv.at[CORE], core).start()
 
         for name, q in timetable(h, near_mine):
-            if name == "column start":
+            if name == "late sum":
+                late_sum()
+            elif name == "column start":
                 column_start()
             elif name == "column middle":
                 column_middle(column, block, x, y, z, k, COL)
             elif name == "far whole":
                 ref = whole(flane, "far", q)
-                arrive(ref, FAR + 2 * q)
+                arrive(late(ref), FAR + 2 * q)
                 copy(late(ref), late(ref), send.at[S_LO], recv.at[LOF + q], lo).start()
                 to_core(ref)
             elif name == "far early":
-                arrive(early(whole(flane, "own", q)), FAR + 2 * q + 1)
+                arrive(panel.at[pl.ds(0, 128), pl.ds(0, EARLY)], FAR + 2 * q + 1)
             elif name == "lo":
                 ref = whole(flane, "own", q)
                 arrive(late(ref), LO + q)
@@ -416,7 +431,7 @@
         sent(S_CORE, got)
         sent(S_LO, sized(512, S - EARLY))
         sent(S_FED, sized(64, EARLY))
-        for n, ref in enumerate((sized(256), sized(256, EARLY))):
+        for n, ref in enumerate((sized(256, S - EARLY), sized(512, EARLY))):
             sent(S_NEAR + n, ref)
             sent(S_FAR + n, ref)
             sent(S_SOURCE + n, ref, hops == 0)

time: 158 us -> 156 us (0.987)
  Pallas kernels: 156 us -> 154 us
    pallas_call x1, Pallas kernels: 156 us -> 154 us  [body(): pl.pallas_call(kernel, out_shape=pltpu.VMEM((2048, 512), F32), in_specs=[...]
where the time goes in v5:
time: 156 us
  Pallas kernels  154 us (99%)
  local copies, waits for them, and re-layouts  2.02 us (1%)
    pallas_call x1, Pallas kernels, body(): pl.pallas_call(kernel, out_shape=pltpu.VMEM((2048, 512), F32), in_specs=[...  154 us

profile of v5, /device:TPU:25, one launch (start us, length us, event | category | flops | bytes accessed | tf_op | source)
XLA Modules:
  0.0 156.2 jit_solution(17642688023900755512)
XLA Ops:
  0.0 154.1 %concord_steps.1 = f32[2048,512]{1,0:T(8,128)S(1)} custom-call(f32[64,384]{1,0:T(8,128)} %bitcast.1, f32[2048,512]{1,0:T(8,128)} %omega_ref.1), custom_call_target="tpu_custom_call" | custom-call | tf_op jit(solution)/shard_map/concord_steps/pallas_call | solution.py:519
  154.2 2.0 %copy.4 = f32[2048,512]{1,0:T(8,128)} copy(f32[2048,512]{1,0:T(8,128)S(1)} %concord_steps.1) | data formatting | bytes 8388608

commit v6 on v5

--- a/solution.py
+++ b/solution.py
@@ -444,15 +444,18 @@
 TILE = 512
 
 
-def update_tile(i, where, count, samples, projected, omega, left, right):
+def set_left(i, ref, left, j):
+    hi, lo = split(ref[rows(i * TILE, TILE)])
+    left[i, :, j * S:(j + 1) * S] = hi
+    left[i, :, (j + 2) * S:(j + 3) * S] = hi
+    left[i, :, (j + 4) * S:(j + 5) * S] = lo
+
+
+def update_tile(i, where, count, projected, omega, left, right):
     x, y, z, k = where
     at = rows(i * TILE, TILE)
-    for j, ref in enumerate((samples, projected)):
-        hi, lo = split(ref[at])
-        left[:, j * S:(j + 1) * S] = hi
-        left[:, (j + 2) * S:(j + 3) * S] = hi
-        left[:, (j + 4) * S:(j + 5) * S] = lo
-    cross = lax.dot_general(left[...], right[...], (((1,), (1,)), ((), ())), preferred_element_type=F32)
+    set_left(i, projected, left, 1)
+    cross = lax.dot_general(left[i], right[...], (((1,), (1,)), ((), ())), preferred_element_type=F32)
     old = omega[at]
     moved = old - (STEP * 0.5 / count) * cross
     threshold = STEP * PENALTY
@@ -490,13 +493,24 @@
         partial_block(zz, acc, flipped, omega, tall)
 
     finish = gather_samples(own_ref, samples, samples_block, projected0, x_send, x_recv, where, partial)
-    finish = gather_projected(acc, part, block0, projected0, inbox0, fed0, send0, recv0, where, finish)
-    set_right(right, samples_block, 1)
+    samples_sent = finish
+
+    def prepare():
+        samples_sent()
+        set_right(right, samples_block, 1)
+
+        def tile(i, _):
+            set_left(i, samples, left, 0)
+            return 0
+
+        lax.fori_loop(0, 2048 // TILE, tile, 0)
+
+    finish = gather_projected(acc, part, block0, projected0, inbox0, fed0, send0, recv0, where, prepare)
     set_right(right, block0, 0)
     acc[...] = jnp.zeros_like(acc)
 
     def first(i, _):
-        update_tile(i, where, S, samples, projected0, omega, left, right)
+        update_tile(i, where, S, projected0, omega, left, right)
         partial_block(2 * i, acc, flipped, omega, tall)
         partial_block(2 * i + 1, acc, flipped, omega, tall)
         return 0
@@ -506,7 +520,7 @@
     set_right(right, block1, 0)
 
     def second(i, _):
-        update_tile(i, where, S, samples, projected1, omega, left, right)
+        update_tile(i, where, S, projected1, omega, left, right)
         return 0
 
     lax.fori_loop(0, 2048 // TILE, second, 0)
@@ -525,7 +539,7 @@
             vmem((2048, S), F32), vmem((512, S), F32), vmem((8, S, 3 * BLOCK), BF16),
             vmem((S, 512), F32), vmem((512, S), F32), vmem((512, S), F32), vmem((2560, S), F32), vmem((2560, S), F32),
             vmem((512, S), F32), vmem((512, S), F32), vmem((7 * 64, S), F32), vmem((7 * 64, S), F32), vmem((256, EARLY), F32), vmem((256, EARLY), F32),
-            vmem((TILE, K3), BF16), vmem((512, K3), BF16), vmem((3 * BLOCK, 512), BF16),
+            vmem((2048 // TILE, TILE, K3), BF16), vmem((512, K3), BF16), vmem((3 * BLOCK, 512), BF16),
             dma((2,)), dma((62,)), dma((SENDS,)), dma((RECVS,)), dma((SENDS,)), dma((RECVS,)), dma,
         ],
         compiler_params=pltpu.CompilerParams(collective_id=0, has_side_effects=True, vmem_limit_bytes=VMEM_LIMIT),

time: 156 us -> 156 us (level)
  no operation moved by 1% of the time
where the time goes in v6:
time: 156 us
  Pallas kernels  154 us (99%)
  local copies, waits for them, and re-layouts  2.02 us (1%)
    pallas_call x1, Pallas kernels, body(): pl.pallas_call(kernel, out_shape=pltpu.VMEM((2048, 512), F32), in_specs=[...  154 us

profile of v6, /device:TPU:25, one launch (start us, length us, event | category | flops | bytes accessed | tf_op | source)
XLA Modules:
  0.0 156.0 jit_solution(62866485062764943)
XLA Ops:
  0.0 154.0 %concord_steps.1 = f32[2048,512]{1,0:T(8,128)S(1)} custom-call(f32[64,384]{1,0:T(8,128)} %bitcast.1, f32[2048,512]{1,0:T(8,128)} %omega_ref.1), custom_call_target="tpu_custom_call" | custom-call | tf_op jit(solution)/shard_map/concord_steps/pallas_call | solution.py:533
  154.0 2.0 %copy.4 = f32[2048,512]{1,0:T(8,128)} copy(f32[2048,512]{1,0:T(8,128)S(1)} %concord_steps.1) | data formatting | bytes 8388608
